TPU v7x, 32 devices: a whole 2x2x4 slice. The times are simulated.
32 devices in a mesh: len: 8 (over y, x, core), wid: 4 (over z).
Axes of the slice: x: 2, y: 2, z: 4, core: 2. Of those that a mesh axis runs over, the one named last changes fastest.
Arguments:
- ckpt_e: float32 [3, 128, 64, 128], P(None, 'len', 'wid'), may hold values from -6 to 6
- ckpt_h: float32 [3, 128, 64, 128], P(None, 'len', 'wid'), may hold values from -6 to 6
- adj_e: float32 [3, 128, 64, 128], P(None, 'len', 'wid'), may hold values from -6 to 6
- adj_h: float32 [3, 128, 64, 128], P(None, 'len', 'wid'), may hold values from -6 to 6
- material: int32 [128, 64, 128], P('len', 'wid'), may hold values from 0 to 3
- inv_perm: float32 [4], replicated, may hold values from 0.2 to 1
- poling: int32 [16, 8], P('len', 'wid'), may hold values from 0 to 1
- freqs: float32 [8], replicated, may hold values from 0.1 to 3
Outputs:
- adjoint_e: float32 [3, 128, 64, 128], P(None, 'len', 'wid')
- adjoint_h: float32 [3, 128, 64, 128], P(None, 'len', 'wid')
- gradient: float32 [2, 8, 16, 8], P(None, None, 'len', 'wid')
All inputs are finite; a program needn't handle non-finite values.
Results may differ from a plain program's by a relative error of at most 0.0001.
Values sent between devices are 32-bit elements; how exact they have to be, the bound alone decides.
A program may use at most 64 MiB of HBM per device.

v0:
```python
import math

import jax
import jax.numpy as jnp
from jax import lax
from jax.sharding import PartitionSpec as P

STEPS = 8
DOMLEN = 8
WBLK = 8


COURANT = 0.5
OMEGA = 0.9


def shifted(value, axis, steps):
    count = lax.axis_size(axis)
    leading, last = (max(0, -steps), min(count, count - steps))
    return lax.ppermute(value, axis, [(source, source + steps) for source in range(leading, last)])


def carried_in(value, axis, join, neutral):
    count, mine = (lax.axis_size(axis), lax.axis_index(axis))
    pieces = lax.all_gather(value, axis)
    total = jnp.full_like(value, 0) + jnp.asarray(neutral, value.dtype)

    def hop(position, total):
        longer = join(total, pieces[position])
        return jnp.where(position < mine, longer, total)

    return lax.fori_loop(0, count - 1, hop, total)


def zdiff_forward(field):
    padded = jnp.pad(field, ((0, 0), (0, 0), (0, 1)))
    return padded[:, :, 1:] - field


def zdiff_backward(field):
    padded = jnp.pad(field, ((0, 0), (0, 0), (1, 0)))
    return field - padded[:, :, :-1]


def xdiff_forward(field, plane):
    return jnp.concatenate([field[1:], plane[None]], axis=0) - field


def ydiff_forward(field, plane):
    return jnp.concatenate([field[:, 1:], plane[:, None]], axis=1) - field


def xdiff_backward(field, plane):
    return field - jnp.concatenate([plane[None], field[:-1]], axis=0)


def ydiff_backward(field, plane):
    return field - jnp.concatenate([plane[:, None], field[:, :-1]], axis=1)


def curl_electric(electric):
    send_len = electric[:, 0]
    send_wid = electric[:, :, 0]
    after_len = shifted(send_len, "len", -1)
    after_wid = shifted(send_wid, "wid", -1)
    ylen_plane, zlen_plane = (after_len[1], after_len[2])
    xwid_plane, zwid_plane = (after_wid[0], after_wid[2])
    comp_x, comp_y, comp_z = (electric[0], electric[1], electric[2])
    return jnp.stack(
        [
            ydiff_forward(comp_z, zwid_plane) - zdiff_forward(comp_y),
            zdiff_forward(comp_x) - xdiff_forward(comp_z, zlen_plane),
            xdiff_forward(comp_y, ylen_plane) - ydiff_forward(comp_x, xwid_plane),
        ]
    )


def curl_magnetic(magnetic):
    send_len = magnetic[:, -1]
    send_wid = magnetic[:, :, -1]
    before_len = shifted(send_len, "len", 1)
    before_wid = shifted(send_wid, "wid", 1)
    ylen_plane, zlen_plane = (before_len[1], before_len[2])
    xwid_plane, zwid_plane = (before_wid[0], before_wid[2])
    comp_x, comp_y, comp_z = (magnetic[0], magnetic[1], magnetic[2])
    return jnp.stack(
        [
            ydiff_backward(comp_z, zwid_plane) - zdiff_backward(comp_y),
            zdiff_backward(comp_x) - xdiff_backward(comp_z, zlen_plane),
            xdiff_backward(comp_y, ylen_plane) - ydiff_backward(comp_x, xwid_plane),
        ]
    )


def add_arrays(earlier, later):
    return earlier + later


def per_device(ckpt_e, ckpt_h, adj_e, adj_h, material, inv_perm, poling, freqs):
    len_cells = material.shape[0]
    wid_cells = material.shape[1]
    depth = material.shape[2]
    inv_eps = jnp.zeros(material.shape, jnp.float32)
    for index in range(inv_perm.shape[0]):
        inv_eps = inv_eps + (material == index).astype(jnp.float32) * inv_perm[index]
    chi = (material == 0).astype(jnp.float32)
    signs = (2 * poling - 1).astype(jnp.float32)
    sign_full = jnp.repeat(jnp.repeat(signs, DOMLEN, axis=0), WBLK, axis=1)
    anchor = lax.axis_index("len") * len_cells
    position = (anchor + jnp.arange(len_cells, dtype=jnp.int32)).astype(jnp.float32)
    phase = math.pi / DOMLEN * position
    terms = jnp.stack([sign_full * jnp.cos(phase)[:, None], sign_full * jnp.sin(phase)[:, None]])
    running = jnp.cumsum(terms, axis=1)
    device_total = running[:, -1]
    prefix = carried_in(device_total, "len", add_arrays, jnp.zeros_like(device_total))
    envelope = (running + prefix[:, None, :]) / math.sqrt(lax.axis_size("len") * len_cells)
    stored = []
    electric, magnetic = (ckpt_e, ckpt_h)
    for moment in range(STEPS):
        magnetic = magnetic - COURANT * curl_electric(electric)
        electric = electric + COURANT * inv_eps * curl_magnetic(magnetic)
        stored.append(electric)
    adjoint_e, adjoint_h = (adj_e, adj_h)
    dom_len = len_cells // DOMLEN
    dom_wid = wid_cells // WBLK
    gradient = jnp.zeros((2, freqs.shape[0], dom_len, dom_wid), jnp.float32)
    scale = 1.0 / math.sqrt(DOMLEN * WBLK * depth)
    for moment in range(STEPS, 0, -1):
        forward_field = stored[moment - 1]
        drive = envelope[0] * math.cos(OMEGA * moment) + envelope[1] * math.sin(OMEGA * moment)
        adjoint_e = adjoint_e + drive[None, :, :, None] * chi * forward_field
        product = chi * jnp.sum(adjoint_e * forward_field, axis=0)
        blocks = product.reshape(dom_len, DOMLEN, dom_wid, WBLK, depth).sum(axis=(1, 3, 4)) * scale
        angles = freqs * moment
        gradient = gradient + jnp.stack(
            [jnp.cos(angles)[:, None, None] * blocks, -jnp.sin(angles)[:, None, None] * blocks]
        )
        adjoint_e = adjoint_e - COURANT * inv_eps * curl_magnetic(adjoint_h)
        adjoint_h = adjoint_h + COURANT * curl_electric(adjoint_e)
    return (adjoint_e, adjoint_h, gradient)


def solution(mesh):
    in_specs = (
        P(None, "len", "wid", None),
        P(None, "len", "wid", None),
        P(None, "len", "wid", None),
        P(None, "len", "wid", None),
        P("len", "wid", None),
        P(),
        P("len", "wid"),
        P(),
    )
    out_specs = (
        P(None, "len", "wid", None),
        P(None, "len", "wid", None),
        P(None, None, "len", "wid"),
    )
    return jax.shard_map(
        per_device, mesh=mesh, in_specs=in_specs, out_specs=out_specs, check_vma=False
    )
```

profile of v0, /device:TPU:5, one launch (start us, length us, event | category | flops | bytes accessed | tf_op | source)
XLA Modules:
  0.0 292.9 jit_solution(6287030330914959182)
XLA Ops:
  3.6 2.7 collective-permute-start.1
  6.4 3.1 %collective-permute-start.33 = (f32[3,16,128]{2,0,1:T(4,128)S(1)}, f32[3,16,128]{2,0,1:T(4,128)S(1)}, u32[]{:S(2)}, u32[]{:S(2)}) collective-permute-start(f32[3,16,128]{2,0,1:T(4,128)S(1)} %bitcast.1300), channel_id=1, source_target_pairs={{0,4},{4,8},{8,12},{12,16},{16,20},{20,24},{24,28},{1,5},{5,9},{9,... | collective-permute-start | bytes 73736 | tf_op jit(solution)/shard_map/ppermute | solution.py:20
  10.7 4.3 %collective-permute-start.32 = (f32[3,16,128]{2,1,0:T(8,128)S(1)}, f32[3,16,128]{2,1,0:T(8,128)S(1)}, u32[]{:S(2)}, u32[]{:S(2)}) collective-permute-start(f32[3,16,128]{2,1,0:T(8,128)S(1)} %slice_bitcast_fusion.164), channel_id=1, source_target_pairs={{0,1},{1,2},{2,3},{4,5},{5,6},{6,7},{8,9},{9,10},{10,11},{12,13},{... | collective-permute-start | bytes 73736 | tf_op jit(solution)/shard_map/ppermute | solution.py:20
  17.2 8.4 %all-gather = f32[16,1,16]{2,1,0:T(1,128)S(1)} all-gather(f32[2,1,16]{2,1,0:T(1,128)S(1)} %slice.2186), channel_id=2, replica_groups=mesh['len'=8,'wid'=4] {'len'}, dimensions={0}, use_global_device_ids=true | all-gather | bytes 1152 | tf_op jit(solution)/shard_map/all_gather | solution.py:25
  28.7 2.9 %broadcast_select_fusion.1 = (f32[16,16,128]{2,0,1:T(8,128)S(1)}, f32[16,16,128]{2,0,1:T(8,128)S(1)}, f32[16,16,128]{2,0,1:T(8,128)S(1)}, f32[16,16,128]{2,0,1:T...) fusion(pred[16,16,128]{2,0,1:T(8,128)(4,1)S(1)} %get-tuple-elem, ...), kind=kLoop, calls=%fused_computation.687 | loop fusion | flops 589824 | bytes 1219600 | tf_op jit(solution)/shard_map/mul | solution.py:131
  33.6 3.2 %collective-permute-start.2 = (f32[3,16,128]{2,1,0:T(8,128)S(1)}, f32[3,16,128]{2,1,0:T(8,128)S(1)}, u32[]{:S(2)}, u32[]{:S(2)}) collective-permute-start(f32[3,16,128]{2,1,0:T(8,128)S(1)} %slice_bitcast_fusion.180), channel_id=1, source_target_pairs={{0,1},{1,2},{2,3},{4,5},{5,6},{6,7},{8,9},{9,10},{10,11},{12,13},{... | collective-permute-start | bytes 73736 | tf_op jit(solution)/shard_map/ppermute | solution.py:20
  37.2 2.6 collective-permute-start.3
  42.7 4.9 %collective-permute-start.5 = (f32[3,16,128]{2,1,0:T(8,128)S(1)}, f32[3,16,128]{2,1,0:T(8,128)S(1)}, u32[]{:S(2)}, u32[]{:S(2)}) collective-permute-start(f32[3,16,128]{2,1,0:T(8,128)S(1)} %slice_bitcast_fusion.179), channel_id=1, source_target_pairs={{4,0},{8,4},{12,8},{16,12},{20,16},{24,20},{28,24},{5,1},{9,5},{13... | collective-permute-start | bytes 73736 | tf_op jit(solution)/shard_map/ppermute | solution.py:20
  49.0 4.4 %collective-permute-start.6 = (f32[3,16,128]{2,1,0:T(8,128)S(1)}, f32[3,16,128]{2,1,0:T(8,128)S(1)}, u32[]{:S(2)}, u32[]{:S(2)}) collective-permute-start(f32[3,16,128]{2,1,0:T(8,128)S(1)} %slice_bitcast_fusion.178), channel_id=1, source_target_pairs={{0,1},{1,2},{2,3},{4,5},{5,6},{6,7},{8,9},{9,10},{10,11},{12,13},{... | collective-permute-start | bytes 73736 | tf_op jit(solution)/shard_map/ppermute | solution.py:20
  53.5 2.1 collective-permute-start.7
  58.9 5.4 %collective-permute-start.9 = (f32[3,16,128]{2,1,0:T(8,128)S(1)}, f32[3,16,128]{2,1,0:T(8,128)S(1)}, u32[]{:S(2)}, u32[]{:S(2)}) collective-permute-start(f32[3,16,128]{2,1,0:T(8,128)S(1)} %slice_bitcast_fusion.176), channel_id=1, source_target_pairs={{4,0},{8,4},{12,8},{16,12},{20,16},{24,20},{28,24},{5,1},{9,5},{13... | collective-permute-start | bytes 73736 | tf_op jit(solution)/shard_map/ppermute | solution.py:20
  65.7 4.3 %collective-permute-start.10 = (f32[3,16,128]{2,1,0:T(8,128)S(1)}, f32[3,16,128]{2,1,0:T(8,128)S(1)}, u32[]{:S(2)}, u32[]{:S(2)}) collective-permute-start(f32[3,16,128]{2,1,0:T(8,128)S(1)} %slice_bitcast_fusion.175), channel_id=1, source_target_pairs={{0,1},{1,2},{2,3},{4,5},{5,6},{6,7},{8,9},{9,10},{10,11},{12,13},{... | collective-permute-start | bytes 73736 | tf_op jit(solution)/shard_map/ppermute | solution.py:20
  74.2 5.4 %collective-permute-start.13 = (f32[3,16,128]{2,1,0:T(8,128)S(1)}, f32[3,16,128]{2,1,0:T(8,128)S(1)}, u32[]{:S(2)}, u32[]{:S(2)}) collective-permute-start(f32[3,16,128]{2,1,0:T(8,128)S(1)} %bitcast.1334), channel_id=1, source_target_pairs={{4,0},{8,4},{12,8},{16,12},{20,16},{24,20},{28,24},{5,1},{9,5},{13... | collective-permute-start | bytes 73736 | tf_op jit(solution)/shard_map/ppermute | solution.py:20
  81.0 3.2 %collective-permute-done.12 = f32[3,16,128]{2,1,0:T(8,128)S(1)} collective-permute-done((f32[3,16,128]{2,1,0:T(8,128)S(1)}, f32[3,16,128]{2,1,0:T(8,128)S(1)}, u32[]{:S(2)}, u32[]{:S(2)}) %collective-permute-start.12) | collective-permute-done | bytes 24608 | tf_op jit(solution)/shard_map/ppermute | solution.py:20
  84.7 3.2 %collective-permute-start.14 = (f32[3,16,128]{2,1,0:T(8,128)S(1)}, f32[3,16,128]{2,1,0:T(8,128)S(1)}, u32[]{:S(2)}, u32[]{:S(2)}) collective-permute-start(f32[3,16,128]{2,1,0:T(8,128)S(1)} %slice_bitcast_fusion.173), channel_id=1, source_target_pairs={{0,1},{1,2},{2,3},{4,5},{5,6},{6,7},{8,9},{9,10},{10,11},{12,13},{... | collective-permute-start | bytes 73736 | tf_op jit(solution)/shard_map/ppermute | solution.py:20
  89.9 2.1 collective-permute-done.15
  92.4 5.4 %collective-permute-start.17 = (f32[3,16,128]{2,1,0:T(8,128)S(1)}, f32[3,16,128]{2,1,0:T(8,128)S(1)}, u32[]{:S(2)}, u32[]{:S(2)}) collective-permute-start(f32[3,16,128]{2,1,0:T(8,128)S(1)} %bitcast.1335), channel_id=1, source_target_pairs={{4,0},{8,4},{12,8},{16,12},{20,16},{24,20},{28,24},{5,1},{9,5},{13... | collective-permute-start | bytes 73736 | tf_op jit(solution)/shard_map/ppermute | solution.py:20
  99.2 3.2 %collective-permute-done.16 = f32[3,16,128]{2,1,0:T(8,128)S(1)} collective-permute-done((f32[3,16,128]{2,1,0:T(8,128)S(1)}, f32[3,16,128]{2,1,0:T(8,128)S(1)}, u32[]{:S(2)}, u32[]{:S(2)}) %collective-permute-start.16) | collective-permute-done | bytes 24608 | tf_op jit(solution)/shard_map/ppermute | solution.py:20
  106.6 2.1 collective-permute-done.19
  109.1 5.4 %collective-permute-start.21 = (f32[3,16,128]{2,1,0:T(8,128)S(1)}, f32[3,16,128]{2,1,0:T(8,128)S(1)}, u32[]{:S(2)}, u32[]{:S(2)}) collective-permute-start(f32[3,16,128]{2,1,0:T(8,128)S(1)} %bitcast.1336), channel_id=1, source_target_pairs={{4,0},{8,4},{12,8},{16,12},{20,16},{24,20},{28,24},{5,1},{9,5},{13... | collective-permute-start | bytes 73736 | tf_op jit(solution)/shard_map/ppermute | solution.py:20
  115.9 3.2 %collective-permute-done.20 = f32[3,16,128]{2,1,0:T(8,128)S(1)} collective-permute-done((f32[3,16,128]{2,1,0:T(8,128)S(1)}, f32[3,16,128]{2,1,0:T(8,128)S(1)}, u32[]{:S(2)}, u32[]{:S(2)}) %collective-permute-start.20) | collective-permute-done | bytes 24608 | tf_op jit(solution)/shard_map/ppermute | solution.py:20
  123.3 2.1 collective-permute-done.23
  125.9 5.4 %collective-permute-start.25 = (f32[3,16,128]{2,1,0:T(8,128)S(1)}, f32[3,16,128]{2,1,0:T(8,128)S(1)}, u32[]{:S(2)}, u32[]{:S(2)}) collective-permute-start(f32[3,16,128]{2,1,0:T(8,128)S(1)} %bitcast.1337), channel_id=1, source_target_pairs={{4,0},{8,4},{12,8},{16,12},{20,16},{24,20},{28,24},{5,1},{9,5},{13... | collective-permute-start | bytes 73736 | tf_op jit(solution)/shard_map/ppermute | solution.py:20
  132.7 3.2 %collective-permute-done.24 = f32[3,16,128]{2,1,0:T(8,128)S(1)} collective-permute-done((f32[3,16,128]{2,1,0:T(8,128)S(1)}, f32[3,16,128]{2,1,0:T(8,128)S(1)}, u32[]{:S(2)}, u32[]{:S(2)}) %collective-permute-start.24) | collective-permute-done | bytes 24608 | tf_op jit(solution)/shard_map/ppermute | solution.py:20
  138.2 2.1 collective-permute-start.27
  142.6 5.4 %collective-permute-start.29 = (f32[3,16,128]{2,1,0:T(8,128)S(1)}, f32[3,16,128]{2,1,0:T(8,128)S(1)}, u32[]{:S(2)}, u32[]{:S(2)}) collective-permute-start(f32[3,16,128]{2,1,0:T(8,128)S(1)} %bitcast.1338), channel_id=1, source_target_pairs={{4,0},{8,4},{12,8},{16,12},{20,16},{24,20},{28,24},{5,1},{9,5},{13... | collective-permute-start | bytes 73736 | tf_op jit(solution)/shard_map/ppermute | solution.py:20
  149.4 3.2 %collective-permute-done.28 = f32[3,16,128]{2,1,0:T(8,128)S(1)} collective-permute-done((f32[3,16,128]{2,1,0:T(8,128)S(1)}, f32[3,16,128]{2,1,0:T(8,128)S(1)}, u32[]{:S(2)}, u32[]{:S(2)}) %collective-permute-start.28) | collective-permute-done | bytes 24608 | tf_op jit(solution)/shard_map/ppermute | solution.py:20
  160.6 4.6 %collective-permute-start.35 = (f32[3,16,128]{2,0,1:T(4,128)S(1)}, f32[3,16,128]{2,0,1:T(4,128)S(1)}, u32[]{:S(2)}, u32[]{:S(2)}) collective-permute-start(f32[3,16,128]{2,0,1:T(4,128)S(1)} %bitcast.1310), channel_id=1, source_target_pairs={{4,0},{8,4},{12,8},{16,12},{20,16},{24,20},{28,24},{5,1},{9,5},{13... | collective-permute-start | bytes 73736 | tf_op jit(solution)/shard_map/ppermute | solution.py:20
  168.5 4.5 %collective-permute-start.36 = (f32[3,16,128]{2,1,0:T(8,128)S(1)}, f32[3,16,128]{2,1,0:T(8,128)S(1)}, u32[]{:S(2)}, u32[]{:S(2)}) collective-permute-start(f32[3,16,128]{2,1,0:T(8,128)S(1)} %slice_bitcast_fusion.162), channel_id=1, source_target_pairs={{0,1},{1,2},{2,3},{4,5},{5,6},{6,7},{8,9},{9,10},{10,11},{12,13},{... | collective-permute-start | bytes 73736 | tf_op jit(solution)/shard_map/ppermute | solution.py:20
  174.4 4.4 %collective-permute-start.39 = (f32[3,16,128]{2,0,1:T(4,128)S(1)}, f32[3,16,128]{2,0,1:T(4,128)S(1)}, u32[]{:S(2)}, u32[]{:S(2)}) collective-permute-start(f32[3,16,128]{2,0,1:T(4,128)S(1)} %bitcast.1312), channel_id=1, source_target_pairs={{4,0},{8,4},{12,8},{16,12},{20,16},{24,20},{28,24},{5,1},{9,5},{13... | collective-permute-start | bytes 73736 | tf_op jit(solution)/shard_map/ppermute | solution.py:20
  180.2 3.8 %collective-permute-done.38 = f32[3,16,128]{2,1,0:T(8,128)S(1)} collective-permute-done((f32[3,16,128]{2,1,0:T(8,128)S(1)}, f32[3,16,128]{2,1,0:T(8,128)S(1)}, u32[]{:S(2)}, u32[]{:S(2)}) %collective-permute-start.38) | collective-permute-done | bytes 24608 | tf_op jit(solution)/shard_map/ppermute | solution.py:20
  186.7 3.5 %collective-permute-start.40 = (f32[3,16,128]{2,1,0:T(8,128)S(1)}, f32[3,16,128]{2,1,0:T(8,128)S(1)}, u32[]{:S(2)}, u32[]{:S(2)}) collective-permute-start(f32[3,16,128]{2,1,0:T(8,128)S(1)} %slice_bitcast_fusion.160), channel_id=1, source_target_pairs={{0,1},{1,2},{2,3},{4,5},{5,6},{6,7},{8,9},{9,10},{10,11},{12,13},{... | collective-permute-start | bytes 73736 | tf_op jit(solution)/shard_map/ppermute | solution.py:20
  191.7 5.3 %collective-permute-start.43 = (f32[3,16,128]{2,0,1:T(4,128)S(1)}, f32[3,16,128]{2,0,1:T(4,128)S(1)}, u32[]{:S(2)}, u32[]{:S(2)}) collective-permute-start(f32[3,16,128]{2,0,1:T(4,128)S(1)} %bitcast.1313), channel_id=1, source_target_pairs={{4,0},{8,4},{12,8},{16,12},{20,16},{24,20},{28,24},{5,1},{9,5},{13... | collective-permute-start | bytes 73736 | tf_op jit(solution)/shard_map/ppermute | solution.py:20
  198.4 3.8 %collective-permute-done.42 = f32[3,16,128]{2,1,0:T(8,128)S(1)} collective-permute-done((f32[3,16,128]{2,1,0:T(8,128)S(1)}, f32[3,16,128]{2,1,0:T(8,128)S(1)}, u32[]{:S(2)}, u32[]{:S(2)}) %collective-permute-start.42) | collective-permute-done | bytes 24608 | tf_op jit(solution)/shard_map/ppermute | solution.py:20
  204.6 3.4 %collective-permute-start.44 = (f32[3,16,128]{2,1,0:T(8,128)S(1)}, f32[3,16,128]{2,1,0:T(8,128)S(1)}, u32[]{:S(2)}, u32[]{:S(2)}) collective-permute-start(f32[3,16,128]{2,1,0:T(8,128)S(1)} %slice_bitcast_fusion.158), channel_id=1, source_target_pairs={{0,1},{1,2},{2,3},{4,5},{5,6},{6,7},{8,9},{9,10},{10,11},{12,13},{... | collective-permute-start | bytes 73736 | tf_op jit(solution)/shard_map/ppermute | solution.py:20
  209.4 5.4 %collective-permute-start.47 = (f32[3,16,128]{2,0,1:T(4,128)S(1)}, f32[3,16,128]{2,0,1:T(4,128)S(1)}, u32[]{:S(2)}, u32[]{:S(2)}) collective-permute-start(f32[3,16,128]{2,0,1:T(4,128)S(1)} %bitcast.1314), channel_id=1, source_target_pairs={{4,0},{8,4},{12,8},{16,12},{20,16},{24,20},{28,24},{5,1},{9,5},{13... | collective-permute-start | bytes 73736 | tf_op jit(solution)/shard_map/ppermute | solution.py:20
  216.1 3.8 %collective-permute-done.46 = f32[3,16,128]{2,1,0:T(8,128)S(1)} collective-permute-done((f32[3,16,128]{2,1,0:T(8,128)S(1)}, f32[3,16,128]{2,1,0:T(8,128)S(1)}, u32[]{:S(2)}, u32[]{:S(2)}) %collective-permute-start.46) | collective-permute-done | bytes 24608 | tf_op jit(solution)/shard_map/ppermute | solution.py:20
  222.5 3.4 %collective-permute-start.48 = (f32[3,16,128]{2,1,0:T(8,128)S(1)}, f32[3,16,128]{2,1,0:T(8,128)S(1)}, u32[]{:S(2)}, u32[]{:S(2)}) collective-permute-start(f32[3,16,128]{2,1,0:T(8,128)S(1)} %slice_bitcast_fusion.156), channel_id=1, source_target_pairs={{0,1},{1,2},{2,3},{4,5},{5,6},{6,7},{8,9},{9,10},{10,11},{12,13},{... | collective-permute-start | bytes 73736 | tf_op jit(solution)/shard_map/ppermute | solution.py:20
  227.3 5.4 %collective-permute-start.51 = (f32[3,16,128]{2,0,1:T(4,128)S(1)}, f32[3,16,128]{2,0,1:T(4,128)S(1)}, u32[]{:S(2)}, u32[]{:S(2)}) collective-permute-start(f32[3,16,128]{2,0,1:T(4,128)S(1)} %bitcast.1315), channel_id=1, source_target_pairs={{4,0},{8,4},{12,8},{16,12},{20,16},{24,20},{28,24},{5,1},{9,5},{13... | collective-permute-start | bytes 73736 | tf_op jit(solution)/shard_map/ppermute | solution.py:20
  234.0 3.8 %collective-permute-done.50 = f32[3,16,128]{2,1,0:T(8,128)S(1)} collective-permute-done((f32[3,16,128]{2,1,0:T(8,128)S(1)}, f32[3,16,128]{2,1,0:T(8,128)S(1)}, u32[]{:S(2)}, u32[]{:S(2)}) %collective-permute-start.50) | collective-permute-done | bytes 24608 | tf_op jit(solution)/shard_map/ppermute | solution.py:20
  240.2 3.4 %collective-permute-start.52 = (f32[3,16,128]{2,1,0:T(8,128)S(1)}, f32[3,16,128]{2,1,0:T(8,128)S(1)}, u32[]{:S(2)}, u32[]{:S(2)}) collective-permute-start(f32[3,16,128]{2,1,0:T(8,128)S(1)} %slice_bitcast_fusion.154), channel_id=1, source_target_pairs={{0,1},{1,2},{2,3},{4,5},{5,6},{6,7},{8,9},{9,10},{10,11},{12,13},{... | collective-permute-start | bytes 73736 | tf_op jit(solution)/shard_map/ppermute | solution.py:20
  245.0 5.4 %collective-permute-start.55 = (f32[3,16,128]{2,0,1:T(4,128)S(1)}, f32[3,16,128]{2,0,1:T(4,128)S(1)}, u32[]{:S(2)}, u32[]{:S(2)}) collective-permute-start(f32[3,16,128]{2,0,1:T(4,128)S(1)} %bitcast.1316), channel_id=1, source_target_pairs={{4,0},{8,4},{12,8},{16,12},{20,16},{24,20},{28,24},{5,1},{9,5},{13... | collective-permute-start | bytes 73736 | tf_op jit(solution)/shard_map/ppermute | solution.py:20
  251.9 3.7 %collective-permute-done.54 = f32[3,16,128]{2,1,0:T(8,128)S(1)} collective-permute-done((f32[3,16,128]{2,1,0:T(8,128)S(1)}, f32[3,16,128]{2,1,0:T(8,128)S(1)}, u32[]{:S(2)}, u32[]{:S(2)}) %collective-permute-start.54) | collective-permute-done | bytes 24608 | tf_op jit(solution)/shard_map/ppermute | solution.py:20
  256.2 3.4 %collective-permute-start.56 = (f32[3,16,128]{2,1,0:T(8,128)S(1)}, f32[3,16,128]{2,1,0:T(8,128)S(1)}, u32[]{:S(2)}, u32[]{:S(2)}) collective-permute-start(f32[3,16,128]{2,1,0:T(8,128)S(1)} %bitcast.1332), channel_id=1, source_target_pairs={{0,1},{1,2},{2,3},{4,5},{5,6},{6,7},{8,9},{9,10},{10,11},{12,13},{... | collective-permute-start | bytes 73736 | tf_op jit(solution)/shard_map/ppermute | solution.py:20
  261.5 3.6 %collective-permute-done.57 = f32[3,16,128]{2,1,0:T(8,128)S(1)} collective-permute-done((f32[3,16,128]{2,1,0:T(8,128)S(1)}, f32[3,16,128]{2,1,0:T(8,128)S(1)}, u32[]{:S(2)}, u32[]{:S(2)}) %collective-permute-start.57) | collective-permute-done | bytes 24608 | tf_op jit(solution)/shard_map/ppermute | solution.py:20
  267.0 5.4 %collective-permute-start.59 = (f32[3,16,128]{2,1,0:T(8,128)S(1)}, f32[3,16,128]{2,1,0:T(8,128)S(1)}, u32[]{:S(2)}, u32[]{:S(2)}) collective-permute-start(f32[3,16,128]{2,1,0:T(8,128)S(1)} %slice_bitcast_fusion.151), channel_id=1, source_target_pairs={{4,0},{8,4},{12,8},{16,12},{20,16},{24,20},{28,24},{5,1},{9,5},{13... | collective-permute-start | bytes 73736 | tf_op jit(solution)/shard_map/ppermute | solution.py:20
  276.7 4.3 %collective-permute-start.60 = (f32[3,16,128]{2,1,0:T(8,128)S(1)}, f32[3,16,128]{2,1,0:T(8,128)S(1)}, u32[]{:S(2)}, u32[]{:S(2)}) collective-permute-start(f32[3,16,128]{2,1,0:T(8,128)S(1)} %bitcast.1333), channel_id=1, source_target_pairs={{0,1},{1,2},{2,3},{4,5},{5,6},{6,7},{8,9},{9,10},{10,11},{12,13},{... | collective-permute-start | bytes 73736 | tf_op jit(solution)/shard_map/ppermute | solution.py:20
  285.8 5.2 %collective-permute-start.63 = (f32[3,16,128]{2,1,0:T(8,128)S(1)}, f32[3,16,128]{2,1,0:T(8,128)S(1)}, u32[]{:S(2)}, u32[]{:S(2)}) collective-permute-start(f32[3,16,128]{2,1,0:T(8,128)S(1)} %slice_bitcast_fusion.149), channel_id=1, source_target_pairs={{4,0},{8,4},{12,8},{16,12},{20,16},{24,20},{28,24},{5,1},{9,5},{13... | collective-permute-start | bytes 73736 | tf_op jit(solution)/shard_map/ppermute | solution.py:20
  (575 shorter events, 96.9 us)
Async XLA Ops:
  1.6 30.7 %collective-permute-start = (f32[3,16,128]{2,1,0:T(8,128)S(1)}, f32[3,16,128]{2,1,0:T(8,128)S(1)}, u32[]{:S(2)}, u32[]{:S(2)}) collective-permute-start(f32[3,16,128]{2,1,0:T(8,128)S(1)} %bitcast.1325), channel_id=1, source_target_pairs={{1,0},{2,1},{3,2},{5,4},{6,5},{7,6},{9,8},{10,9},{11,10},{13,12},{... | collective-permute-start | bytes 73736 | tf_op jit(solution)/shard_map/ppermute | solution.py:20
  3.6 28.6 %collective-permute-start.1 = (f32[3,16,128]{2,1,0:T(8,128)S(1)}, f32[3,16,128]{2,1,0:T(8,128)S(1)}, u32[]{:S(2)}, u32[]{:S(2)}) collective-permute-start(f32[3,16,128]{2,1,0:T(8,128)S(1)} %slice_bitcast_fusion.181), channel_id=1, source_target_pairs={{4,0},{8,4},{12,8},{16,12},{20,16},{24,20},{28,24},{5,1},{9,5},{13... | collective-permute-start | bytes 73736 | tf_op jit(solution)/shard_map/ppermute | solution.py:20
  6.4 30.4 %collective-permute-start.33 = (f32[3,16,128]{2,0,1:T(4,128)S(1)}, f32[3,16,128]{2,0,1:T(4,128)S(1)}, u32[]{:S(2)}, u32[]{:S(2)}) collective-permute-start(f32[3,16,128]{2,0,1:T(4,128)S(1)} %bitcast.1300), channel_id=1, source_target_pairs={{0,4},{4,8},{8,12},{12,16},{16,20},{20,24},{24,28},{1,5},{5,9},{9,... | collective-permute-start | bytes 73736 | tf_op jit(solution)/shard_map/ppermute | solution.py:20
  10.7 26.2 %collective-permute-start.32 = (f32[3,16,128]{2,1,0:T(8,128)S(1)}, f32[3,16,128]{2,1,0:T(8,128)S(1)}, u32[]{:S(2)}, u32[]{:S(2)}) collective-permute-start(f32[3,16,128]{2,1,0:T(8,128)S(1)} %slice_bitcast_fusion.164), channel_id=1, source_target_pairs={{0,1},{1,2},{2,3},{4,5},{5,6},{6,7},{8,9},{9,10},{10,11},{12,13},{... | collective-permute-start | bytes 73736 | tf_op jit(solution)/shard_map/ppermute | solution.py:20
  33.6 6.2 %collective-permute-start.2 = (f32[3,16,128]{2,1,0:T(8,128)S(1)}, f32[3,16,128]{2,1,0:T(8,128)S(1)}, u32[]{:S(2)}, u32[]{:S(2)}) collective-permute-start(f32[3,16,128]{2,1,0:T(8,128)S(1)} %slice_bitcast_fusion.180), channel_id=1, source_target_pairs={{0,1},{1,2},{2,3},{4,5},{5,6},{6,7},{8,9},{9,10},{10,11},{12,13},{... | collective-permute-start | bytes 73736 | tf_op jit(solution)/shard_map/ppermute | solution.py:20
  41.4 6.5 %collective-permute-start.4 = (f32[3,16,128]{2,1,0:T(8,128)S(1)}, f32[3,16,128]{2,1,0:T(8,128)S(1)}, u32[]{:S(2)}, u32[]{:S(2)}) collective-permute-start(f32[3,16,128]{2,1,0:T(8,128)S(1)} %bitcast.1327), channel_id=1, source_target_pairs={{1,0},{2,1},{3,2},{5,4},{6,5},{7,6},{9,8},{10,9},{11,10},{13,12},{... | collective-permute-start | bytes 73736 | tf_op jit(solution)/shard_map/ppermute | solution.py:20
  42.7 5.7 %collective-permute-start.5 = (f32[3,16,128]{2,1,0:T(8,128)S(1)}, f32[3,16,128]{2,1,0:T(8,128)S(1)}, u32[]{:S(2)}, u32[]{:S(2)}) collective-permute-start(f32[3,16,128]{2,1,0:T(8,128)S(1)} %slice_bitcast_fusion.179), channel_id=1, source_target_pairs={{4,0},{8,4},{12,8},{16,12},{20,16},{24,20},{28,24},{5,1},{9,5},{13... | collective-permute-start | bytes 73736 | tf_op jit(solution)/shard_map/ppermute | solution.py:20
  49.0 6.6 %collective-permute-start.6 = (f32[3,16,128]{2,1,0:T(8,128)S(1)}, f32[3,16,128]{2,1,0:T(8,128)S(1)}, u32[]{:S(2)}, u32[]{:S(2)}) collective-permute-start(f32[3,16,128]{2,1,0:T(8,128)S(1)} %slice_bitcast_fusion.178), channel_id=1, source_target_pairs={{0,1},{1,2},{2,3},{4,5},{5,6},{6,7},{8,9},{9,10},{10,11},{12,13},{... | collective-permute-start | bytes 73736 | tf_op jit(solution)/shard_map/ppermute | solution.py:20
  57.5 7.0 %collective-permute-start.8 = (f32[3,16,128]{2,1,0:T(8,128)S(1)}, f32[3,16,128]{2,1,0:T(8,128)S(1)}, u32[]{:S(2)}, u32[]{:S(2)}) collective-permute-start(f32[3,16,128]{2,1,0:T(8,128)S(1)} %slice_bitcast_fusion.177), channel_id=1, source_target_pairs={{1,0},{2,1},{3,2},{5,4},{6,5},{7,6},{9,8},{10,9},{11,10},{13,12},{... | collective-permute-start | bytes 73736 | tf_op jit(solution)/shard_map/ppermute | solution.py:20
  58.9 6.3 %collective-permute-start.9 = (f32[3,16,128]{2,1,0:T(8,128)S(1)}, f32[3,16,128]{2,1,0:T(8,128)S(1)}, u32[]{:S(2)}, u32[]{:S(2)}) collective-permute-start(f32[3,16,128]{2,1,0:T(8,128)S(1)} %slice_bitcast_fusion.176), channel_id=1, source_target_pairs={{4,0},{8,4},{12,8},{16,12},{20,16},{24,20},{28,24},{5,1},{9,5},{13... | collective-permute-start | bytes 73736 | tf_op jit(solution)/shard_map/ppermute | solution.py:20
  65.7 6.3 %collective-permute-start.10 = (f32[3,16,128]{2,1,0:T(8,128)S(1)}, f32[3,16,128]{2,1,0:T(8,128)S(1)}, u32[]{:S(2)}, u32[]{:S(2)}) collective-permute-start(f32[3,16,128]{2,1,0:T(8,128)S(1)} %slice_bitcast_fusion.175), channel_id=1, source_target_pairs={{0,1},{1,2},{2,3},{4,5},{5,6},{6,7},{8,9},{9,10},{10,11},{12,13},{... | collective-permute-start | bytes 73736 | tf_op jit(solution)/shard_map/ppermute | solution.py:20
  74.2 6.8 %collective-permute-start.13 = (f32[3,16,128]{2,1,0:T(8,128)S(1)}, f32[3,16,128]{2,1,0:T(8,128)S(1)}, u32[]{:S(2)}, u32[]{:S(2)}) collective-permute-start(f32[3,16,128]{2,1,0:T(8,128)S(1)} %bitcast.1334), channel_id=1, source_target_pairs={{4,0},{8,4},{12,8},{16,12},{20,16},{24,20},{28,24},{5,1},{9,5},{13... | collective-permute-start | bytes 73736 | tf_op jit(solution)/shard_map/ppermute | solution.py:20
  79.6 4.6 %collective-permute-start.12 = (f32[3,16,128]{2,1,0:T(8,128)S(1)}, f32[3,16,128]{2,1,0:T(8,128)S(1)}, u32[]{:S(2)}, u32[]{:S(2)}) collective-permute-start(f32[3,16,128]{2,1,0:T(8,128)S(1)} %slice_bitcast_fusion.174), channel_id=1, source_target_pairs={{1,0},{2,1},{3,2},{5,4},{6,5},{7,6},{9,8},{10,9},{11,10},{13,12},{... | collective-permute-start | bytes 73736 | tf_op jit(solution)/shard_map/ppermute | solution.py:20
  84.7 5.2 %collective-permute-start.14 = (f32[3,16,128]{2,1,0:T(8,128)S(1)}, f32[3,16,128]{2,1,0:T(8,128)S(1)}, u32[]{:S(2)}, u32[]{:S(2)}) collective-permute-start(f32[3,16,128]{2,1,0:T(8,128)S(1)} %slice_bitcast_fusion.173), channel_id=1, source_target_pairs={{0,1},{1,2},{2,3},{4,5},{5,6},{6,7},{8,9},{9,10},{10,11},{12,13},{... | collective-permute-start | bytes 73736 | tf_op jit(solution)/shard_map/ppermute | solution.py:20
  92.4 6.8 %collective-permute-start.17 = (f32[3,16,128]{2,1,0:T(8,128)S(1)}, f32[3,16,128]{2,1,0:T(8,128)S(1)}, u32[]{:S(2)}, u32[]{:S(2)}) collective-permute-start(f32[3,16,128]{2,1,0:T(8,128)S(1)} %bitcast.1335), channel_id=1, source_target_pairs={{4,0},{8,4},{12,8},{16,12},{20,16},{24,20},{28,24},{5,1},{9,5},{13... | collective-permute-start | bytes 73736 | tf_op jit(solution)/shard_map/ppermute | solution.py:20
  97.9 4.6 %collective-permute-start.16 = (f32[3,16,128]{2,1,0:T(8,128)S(1)}, f32[3,16,128]{2,1,0:T(8,128)S(1)}, u32[]{:S(2)}, u32[]{:S(2)}) collective-permute-start(f32[3,16,128]{2,1,0:T(8,128)S(1)} %slice_bitcast_fusion.172), channel_id=1, source_target_pairs={{1,0},{2,1},{3,2},{5,4},{6,5},{7,6},{9,8},{10,9},{11,10},{13,12},{... | collective-permute-start | bytes 73736 | tf_op jit(solution)/shard_map/ppermute | solution.py:20
  109.1 6.8 %collective-permute-start.21 = (f32[3,16,128]{2,1,0:T(8,128)S(1)}, f32[3,16,128]{2,1,0:T(8,128)S(1)}, u32[]{:S(2)}, u32[]{:S(2)}) collective-permute-start(f32[3,16,128]{2,1,0:T(8,128)S(1)} %bitcast.1336), channel_id=1, source_target_pairs={{4,0},{8,4},{12,8},{16,12},{20,16},{24,20},{28,24},{5,1},{9,5},{13... | collective-permute-start | bytes 73736 | tf_op jit(solution)/shard_map/ppermute | solution.py:20
  114.6 4.6 %collective-permute-start.20 = (f32[3,16,128]{2,1,0:T(8,128)S(1)}, f32[3,16,128]{2,1,0:T(8,128)S(1)}, u32[]{:S(2)}, u32[]{:S(2)}) collective-permute-start(f32[3,16,128]{2,1,0:T(8,128)S(1)} %slice_bitcast_fusion.170), channel_id=1, source_target_pairs={{1,0},{2,1},{3,2},{5,4},{6,5},{7,6},{9,8},{10,9},{11,10},{13,12},{... | collective-permute-start | bytes 73736 | tf_op jit(solution)/shard_map/ppermute | solution.py:20
  125.9 6.8 %collective-permute-start.25 = (f32[3,16,128]{2,1,0:T(8,128)S(1)}, f32[3,16,128]{2,1,0:T(8,128)S(1)}, u32[]{:S(2)}, u32[]{:S(2)}) collective-permute-start(f32[3,16,128]{2,1,0:T(8,128)S(1)} %bitcast.1337), channel_id=1, source_target_pairs={{4,0},{8,4},{12,8},{16,12},{20,16},{24,20},{28,24},{5,1},{9,5},{13... | collective-permute-start | bytes 73736 | tf_op jit(solution)/shard_map/ppermute | solution.py:20
  131.3 4.6 %collective-permute-start.24 = (f32[3,16,128]{2,1,0:T(8,128)S(1)}, f32[3,16,128]{2,1,0:T(8,128)S(1)}, u32[]{:S(2)}, u32[]{:S(2)}) collective-permute-start(f32[3,16,128]{2,1,0:T(8,128)S(1)} %slice_bitcast_fusion.168), channel_id=1, source_target_pairs={{1,0},{2,1},{3,2},{5,4},{6,5},{7,6},{9,8},{10,9},{11,10},{13,12},{... | collective-permute-start | bytes 73736 | tf_op jit(solution)/shard_map/ppermute | solution.py:20
  142.6 6.8 %collective-permute-start.29 = (f32[3,16,128]{2,1,0:T(8,128)S(1)}, f32[3,16,128]{2,1,0:T(8,128)S(1)}, u32[]{:S(2)}, u32[]{:S(2)}) collective-permute-start(f32[3,16,128]{2,1,0:T(8,128)S(1)} %bitcast.1338), channel_id=1, source_target_pairs={{4,0},{8,4},{12,8},{16,12},{20,16},{24,20},{28,24},{5,1},{9,5},{13... | collective-permute-start | bytes 73736 | tf_op jit(solution)/shard_map/ppermute | solution.py:20
  148.1 4.6 %collective-permute-start.28 = (f32[3,16,128]{2,1,0:T(8,128)S(1)}, f32[3,16,128]{2,1,0:T(8,128)S(1)}, u32[]{:S(2)}, u32[]{:S(2)}) collective-permute-start(f32[3,16,128]{2,1,0:T(8,128)S(1)} %slice_bitcast_fusion.166), channel_id=1, source_target_pairs={{1,0},{2,1},{3,2},{5,4},{6,5},{7,6},{9,8},{10,9},{11,10},{13,12},{... | collective-permute-start | bytes 73736 | tf_op jit(solution)/shard_map/ppermute | solution.py:20
  159.3 6.0 %collective-permute-start.34 = (f32[3,16,128]{2,1,0:T(8,128)S(1)}, f32[3,16,128]{2,1,0:T(8,128)S(1)}, u32[]{:S(2)}, u32[]{:S(2)}) collective-permute-start(f32[3,16,128]{2,1,0:T(8,128)S(1)} %slice_bitcast_fusion.163), channel_id=1, source_target_pairs={{1,0},{2,1},{3,2},{5,4},{6,5},{7,6},{9,8},{10,9},{11,10},{13,12},{... | collective-permute-start | bytes 73736 | tf_op jit(solution)/shard_map/ppermute | solution.py:20
  160.6 5.4 %collective-permute-start.35 = (f32[3,16,128]{2,0,1:T(4,128)S(1)}, f32[3,16,128]{2,0,1:T(4,128)S(1)}, u32[]{:S(2)}, u32[]{:S(2)}) collective-permute-start(f32[3,16,128]{2,0,1:T(4,128)S(1)} %bitcast.1310), channel_id=1, source_target_pairs={{4,0},{8,4},{12,8},{16,12},{20,16},{24,20},{28,24},{5,1},{9,5},{13... | collective-permute-start | bytes 73736 | tf_op jit(solution)/shard_map/ppermute | solution.py:20
  166.6 6.5 %collective-permute-start.37 = (f32[3,16,128]{2,0,1:T(4,128)S(1)}, f32[3,16,128]{2,0,1:T(4,128)S(1)}, u32[]{:S(2)}, u32[]{:S(2)}) collective-permute-start(f32[3,16,128]{2,0,1:T(4,128)S(1)} %bitcast.1311), channel_id=1, source_target_pairs={{0,4},{4,8},{8,12},{12,16},{16,20},{20,24},{24,28},{1,5},{5,9},{9,... | collective-permute-start | bytes 73736 | tf_op jit(solution)/shard_map/ppermute | solution.py:20
  168.5 5.4 %collective-permute-start.36 = (f32[3,16,128]{2,1,0:T(8,128)S(1)}, f32[3,16,128]{2,1,0:T(8,128)S(1)}, u32[]{:S(2)}, u32[]{:S(2)}) collective-permute-start(f32[3,16,128]{2,1,0:T(8,128)S(1)} %slice_bitcast_fusion.162), channel_id=1, source_target_pairs={{0,1},{1,2},{2,3},{4,5},{5,6},{6,7},{8,9},{9,10},{10,11},{12,13},{... | collective-permute-start | bytes 73736 | tf_op jit(solution)/shard_map/ppermute | solution.py:20
  174.4 5.7 %collective-permute-start.39 = (f32[3,16,128]{2,0,1:T(4,128)S(1)}, f32[3,16,128]{2,0,1:T(4,128)S(1)}, u32[]{:S(2)}, u32[]{:S(2)}) collective-permute-start(f32[3,16,128]{2,0,1:T(4,128)S(1)} %bitcast.1312), channel_id=1, source_target_pairs={{4,0},{8,4},{12,8},{16,12},{20,16},{24,20},{28,24},{5,1},{9,5},{13... | collective-permute-start | bytes 73736 | tf_op jit(solution)/shard_map/ppermute | solution.py:20
  178.8 5.1 %collective-permute-start.38 = (f32[3,16,128]{2,1,0:T(8,128)S(1)}, f32[3,16,128]{2,1,0:T(8,128)S(1)}, u32[]{:S(2)}, u32[]{:S(2)}) collective-permute-start(f32[3,16,128]{2,1,0:T(8,128)S(1)} %slice_bitcast_fusion.161), channel_id=1, source_target_pairs={{1,0},{2,1},{3,2},{5,4},{6,5},{7,6},{9,8},{10,9},{11,10},{13,12},{... | collective-permute-start | bytes 73736 | tf_op jit(solution)/shard_map/ppermute | solution.py:20
  184.7 5.5 %collective-permute-start.41 = (f32[3,16,128]{2,0,1:T(4,128)S(1)}, f32[3,16,128]{2,0,1:T(4,128)S(1)}, u32[]{:S(2)}, u32[]{:S(2)}) collective-permute-start(f32[3,16,128]{2,0,1:T(4,128)S(1)} %bitcast.1302), channel_id=1, source_target_pairs={{0,4},{4,8},{8,12},{12,16},{16,20},{20,24},{24,28},{1,5},{5,9},{9,... | collective-permute-start | bytes 73736 | tf_op jit(solution)/shard_map/ppermute | solution.py:20
  186.7 4.4 %collective-permute-start.40 = (f32[3,16,128]{2,1,0:T(8,128)S(1)}, f32[3,16,128]{2,1,0:T(8,128)S(1)}, u32[]{:S(2)}, u32[]{:S(2)}) collective-permute-start(f32[3,16,128]{2,1,0:T(8,128)S(1)} %slice_bitcast_fusion.160), channel_id=1, source_target_pairs={{0,1},{1,2},{2,3},{4,5},{5,6},{6,7},{8,9},{9,10},{10,11},{12,13},{... | collective-permute-start | bytes 73736 | tf_op jit(solution)/shard_map/ppermute | solution.py:20
  191.7 6.6 %collective-permute-start.43 = (f32[3,16,128]{2,0,1:T(4,128)S(1)}, f32[3,16,128]{2,0,1:T(4,128)S(1)}, u32[]{:S(2)}, u32[]{:S(2)}) collective-permute-start(f32[3,16,128]{2,0,1:T(4,128)S(1)} %bitcast.1313), channel_id=1, source_target_pairs={{4,0},{8,4},{12,8},{16,12},{20,16},{24,20},{28,24},{5,1},{9,5},{13... | collective-permute-start | bytes 73736 | tf_op jit(solution)/shard_map/ppermute | solution.py:20
  197.0 5.1 %collective-permute-start.42 = (f32[3,16,128]{2,1,0:T(8,128)S(1)}, f32[3,16,128]{2,1,0:T(8,128)S(1)}, u32[]{:S(2)}, u32[]{:S(2)}) collective-permute-start(f32[3,16,128]{2,1,0:T(8,128)S(1)} %slice_bitcast_fusion.159), channel_id=1, source_target_pairs={{1,0},{2,1},{3,2},{5,4},{6,5},{7,6},{9,8},{10,9},{11,10},{13,12},{... | collective-permute-start | bytes 73736 | tf_op jit(solution)/shard_map/ppermute | solution.py:20
  202.6 5.3 %collective-permute-start.45 = (f32[3,16,128]{2,1,0:T(8,128)S(1)}, f32[3,16,128]{2,1,0:T(8,128)S(1)}, u32[]{:S(2)}, u32[]{:S(2)}) collective-permute-start(f32[3,16,128]{2,1,0:T(8,128)S(1)} %bitcast.1329), channel_id=1, source_target_pairs={{0,4},{4,8},{8,12},{12,16},{16,20},{20,24},{24,28},{1,5},{5,9},{9,... | collective-permute-start | bytes 73736 | tf_op jit(solution)/shard_map/ppermute | solution.py:20
  209.4 6.7 %collective-permute-start.47 = (f32[3,16,128]{2,0,1:T(4,128)S(1)}, f32[3,16,128]{2,0,1:T(4,128)S(1)}, u32[]{:S(2)}, u32[]{:S(2)}) collective-permute-start(f32[3,16,128]{2,0,1:T(4,128)S(1)} %bitcast.1314), channel_id=1, source_target_pairs={{4,0},{8,4},{12,8},{16,12},{20,16},{24,20},{28,24},{5,1},{9,5},{13... | collective-permute-start | bytes 73736 | tf_op jit(solution)/shard_map/ppermute | solution.py:20
  214.8 5.1 %collective-permute-start.46 = (f32[3,16,128]{2,1,0:T(8,128)S(1)}, f32[3,16,128]{2,1,0:T(8,128)S(1)}, u32[]{:S(2)}, u32[]{:S(2)}) collective-permute-start(f32[3,16,128]{2,1,0:T(8,128)S(1)} %slice_bitcast_fusion.157), channel_id=1, source_target_pairs={{1,0},{2,1},{3,2},{5,4},{6,5},{7,6},{9,8},{10,9},{11,10},{13,12},{... | collective-permute-start | bytes 73736 | tf_op jit(solution)/shard_map/ppermute | solution.py:20
  220.5 5.4 %collective-permute-start.49 = (f32[3,16,128]{2,0,1:T(4,128)S(1)}, f32[3,16,128]{2,0,1:T(4,128)S(1)}, u32[]{:S(2)}, u32[]{:S(2)}) collective-permute-start(f32[3,16,128]{2,0,1:T(4,128)S(1)} %bitcast.1301), channel_id=1, source_target_pairs={{0,4},{4,8},{8,12},{12,16},{16,20},{20,24},{24,28},{1,5},{5,9},{9,... | collective-permute-start | bytes 73736 | tf_op jit(solution)/shard_map/ppermute | solution.py:20
  227.3 6.7 %collective-permute-start.51 = (f32[3,16,128]{2,0,1:T(4,128)S(1)}, f32[3,16,128]{2,0,1:T(4,128)S(1)}, u32[]{:S(2)}, u32[]{:S(2)}) collective-permute-start(f32[3,16,128]{2,0,1:T(4,128)S(1)} %bitcast.1315), channel_id=1, source_target_pairs={{4,0},{8,4},{12,8},{16,12},{20,16},{24,20},{28,24},{5,1},{9,5},{13... | collective-permute-start | bytes 73736 | tf_op jit(solution)/shard_map/ppermute | solution.py:20
  232.7 5.1 %collective-permute-start.50 = (f32[3,16,128]{2,1,0:T(8,128)S(1)}, f32[3,16,128]{2,1,0:T(8,128)S(1)}, u32[]{:S(2)}, u32[]{:S(2)}) collective-permute-start(f32[3,16,128]{2,1,0:T(8,128)S(1)} %slice_bitcast_fusion.155), channel_id=1, source_target_pairs={{1,0},{2,1},{3,2},{5,4},{6,5},{7,6},{9,8},{10,9},{11,10},{13,12},{... | collective-permute-start | bytes 73736 | tf_op jit(solution)/shard_map/ppermute | solution.py:20
  238.2 5.3 %collective-permute-start.53 = (f32[3,16,128]{2,1,0:T(8,128)S(1)}, f32[3,16,128]{2,1,0:T(8,128)S(1)}, u32[]{:S(2)}, u32[]{:S(2)}) collective-permute-start(f32[3,16,128]{2,1,0:T(8,128)S(1)} %bitcast.1330), channel_id=1, source_target_pairs={{0,4},{4,8},{8,12},{12,16},{16,20},{20,24},{24,28},{1,5},{5,9},{9,... | collective-permute-start | bytes 73736 | tf_op jit(solution)/shard_map/ppermute | solution.py:20
  245.0 6.8 %collective-permute-start.55 = (f32[3,16,128]{2,0,1:T(4,128)S(1)}, f32[3,16,128]{2,0,1:T(4,128)S(1)}, u32[]{:S(2)}, u32[]{:S(2)}) collective-permute-start(f32[3,16,128]{2,0,1:T(4,128)S(1)} %bitcast.1316), channel_id=1, source_target_pairs={{4,0},{8,4},{12,8},{16,12},{20,16},{24,20},{28,24},{5,1},{9,5},{13... | collective-permute-start | bytes 73736 | tf_op jit(solution)/shard_map/ppermute | solution.py:20
  250.5 5.1 %collective-permute-start.54 = (f32[3,16,128]{2,1,0:T(8,128)S(1)}, f32[3,16,128]{2,1,0:T(8,128)S(1)}, u32[]{:S(2)}, u32[]{:S(2)}) collective-permute-start(f32[3,16,128]{2,1,0:T(8,128)S(1)} %slice_bitcast_fusion.153), channel_id=1, source_target_pairs={{1,0},{2,1},{3,2},{5,4},{6,5},{7,6},{9,8},{10,9},{11,10},{13,12},{... | collective-permute-start | bytes 73736 | tf_op jit(solution)/shard_map/ppermute | solution.py:20
  256.2 5.3 %collective-permute-start.56 = (f32[3,16,128]{2,1,0:T(8,128)S(1)}, f32[3,16,128]{2,1,0:T(8,128)S(1)}, u32[]{:S(2)}, u32[]{:S(2)}) collective-permute-start(f32[3,16,128]{2,1,0:T(8,128)S(1)} %bitcast.1332), channel_id=1, source_target_pairs={{0,1},{1,2},{2,3},{4,5},{5,6},{6,7},{8,9},{9,10},{10,11},{12,13},{... | collective-permute-start | bytes 73736 | tf_op jit(solution)/shard_map/ppermute | solution.py:20
  259.6 5.5 %collective-permute-start.57 = (f32[3,16,128]{2,1,0:T(8,128)S(1)}, f32[3,16,128]{2,1,0:T(8,128)S(1)}, u32[]{:S(2)}, u32[]{:S(2)}) collective-permute-start(f32[3,16,128]{2,1,0:T(8,128)S(1)} %slice_bitcast_fusion.152), channel_id=1, source_target_pairs={{0,4},{4,8},{8,12},{12,16},{16,20},{20,24},{24,28},{1,5},{5,9},{9,... | collective-permute-start | bytes 73736 | tf_op jit(solution)/shard_map/ppermute | solution.py:20
  265.7 10.5 %collective-permute-start.58 = (f32[3,16,128]{2,1,0:T(8,128)S(1)}, f32[3,16,128]{2,1,0:T(8,128)S(1)}, u32[]{:S(2)}, u32[]{:S(2)}) collective-permute-start(f32[3,16,128]{2,1,0:T(8,128)S(1)} %bitcast.1326), channel_id=1, source_target_pairs={{1,0},{2,1},{3,2},{5,4},{6,5},{7,6},{9,8},{10,9},{11,10},{13,12},{... | collective-permute-start | bytes 73736 | tf_op jit(solution)/shard_map/ppermute | solution.py:20
  267.0 9.2 %collective-permute-start.59 = (f32[3,16,128]{2,1,0:T(8,128)S(1)}, f32[3,16,128]{2,1,0:T(8,128)S(1)}, u32[]{:S(2)}, u32[]{:S(2)}) collective-permute-start(f32[3,16,128]{2,1,0:T(8,128)S(1)} %slice_bitcast_fusion.151), channel_id=1, source_target_pairs={{4,0},{8,4},{12,8},{16,12},{20,16},{24,20},{28,24},{5,1},{9,5},{13... | collective-permute-start | bytes 73736 | tf_op jit(solution)/shard_map/ppermute | solution.py:20
  276.7 6.2 %collective-permute-start.60 = (f32[3,16,128]{2,1,0:T(8,128)S(1)}, f32[3,16,128]{2,1,0:T(8,128)S(1)}, u32[]{:S(2)}, u32[]{:S(2)}) collective-permute-start(f32[3,16,128]{2,1,0:T(8,128)S(1)} %bitcast.1333), channel_id=1, source_target_pairs={{0,1},{1,2},{2,3},{4,5},{5,6},{6,7},{8,9},{9,10},{10,11},{12,13},{... | collective-permute-start | bytes 73736 | tf_op jit(solution)/shard_map/ppermute | solution.py:20
  284.4 6.5 %collective-permute-start.62 = (f32[3,16,128]{2,1,0:T(8,128)S(1)}, f32[3,16,128]{2,1,0:T(8,128)S(1)}, u32[]{:S(2)}, u32[]{:S(2)}) collective-permute-start(f32[3,16,128]{2,1,0:T(8,128)S(1)} %bitcast.1331), channel_id=1, source_target_pairs={{1,0},{2,1},{3,2},{5,4},{6,5},{7,6},{9,8},{10,9},{11,10},{13,12},{... | collective-permute-start | bytes 73736 | tf_op jit(solution)/shard_map/ppermute | solution.py:20
  285.8 6.0 %collective-permute-start.63 = (f32[3,16,128]{2,1,0:T(8,128)S(1)}, f32[3,16,128]{2,1,0:T(8,128)S(1)}, u32[]{:S(2)}, u32[]{:S(2)}) collective-permute-start(f32[3,16,128]{2,1,0:T(8,128)S(1)} %slice_bitcast_fusion.149), channel_id=1, source_target_pairs={{4,0},{8,4},{12,8},{16,12},{20,16},{24,20},{28,24},{5,1},{9,5},{13... | collective-permute-start | bytes 73736 | tf_op jit(solution)/shard_map/ppermute | solution.py:20
  (26 other events, 87.2 us)
where the time goes:
time: 298 us; the launch traced here: 293 us
  starting transfers between devices  186 us (62%)
  waiting for transfers between devices  60 us (20%)
  other arithmetic  19.2 us (6%)
  local copies, waits for them, and re-layouts  14.8 us (5%)
  blocking collectives  8.36 us (3%)
  between operations  4.01 us (1%)
    ppermute x64, starting transfers between devices, shifted(): lax.ppermute(value, axis, [(source, source + steps) for source in range(l...  186 us
    ppermute x64, waiting for transfers between devices, shifted(): lax.ppermute(value, axis, [(source, source + steps) for source in range(l...  60 us
    all_gather x1, blocking collectives, carried_in(): pieces = lax.all_gather(value, axis)  8.36 us
    unnamed x55, local copies, waits for them, and re-layouts  6.57 us
  transfers between devices with their start and end apart: 64, of which 30 were waited for; matrix products, arithmetic and copies ran while one was open for 5% of the time, Pallas kernels for 0%

commit v1 on v0

v1 whole, which is shorter than its diff:
```python
import math

import jax
import jax.numpy as jnp
from jax import lax
from jax.experimental import pallas as pl
from jax.experimental.pallas import tpu as pltpu
from jax.sharding import PartitionSpec as P

STEPS = 8
DOMLEN = 8
WBLK = 8
COURANT = 0.5
OMEGA = 0.9
MESH = pl.DeviceIdType.MESH
LO = 8
VERSIONS = 2 * STEPS + 1


def zforward(value, lane):
    depth = value.shape[-1]
    return jnp.where(lane < depth - 1, pltpu.roll(value, depth - 1, 1), 0.0)


def zbackward(value, lane):
    return jnp.where(lane > 0, pltpu.roll(value, 1, 1), 0.0)


def make_kernel(count, wcount, nx, ny, nz, bins, nmat):
    top = LO + ny
    dom_len, dom_wid = nx // DOMLEN, ny // WBLK
    span = count * nx

    def kernel(
        ckpt_e, ckpt_h, adj_e, adj_h, material, inv_perm, poling, freqs,
        out_e, out_h, out_g,
        fields, mags, coef, envc, prods, pre, pre_out,
        ysend_hi, ysend_lo, yrecv_lo, yrecv_hi, hsend, hrecv,
        send_sem, recv_sem, hsend_sem, hrecv_sem, psend_sem, precv_sem,
    ):
        me, row = lax.axis_index("len"), lax.axis_index("wid")
        has_prev, has_next = me > 0, me < count - 1
        has_low, has_high = row > 0, row < wcount - 1
        own = pl.ds(LO, ny)

        for v in range(VERSIONS):
            if v == STEPS:
                continue
            for c in range(3):
                fields[v, c, 0, own] = jnp.zeros((ny, nz), jnp.float32)
                fields[v, c, nx + 1, own] = jnp.zeros((ny, nz), jnp.float32)
            fields[v, 0, 0, pl.ds(top, 8)] = jnp.zeros((8, nz), jnp.float32)
            fields[v, 1, nx + 1, pl.ds(0, LO)] = jnp.zeros((LO, nz), jnp.float32)
            yrecv_lo[v] = jnp.zeros((3, nx, nz), jnp.float32)
            yrecv_hi[v] = jnp.zeros((2, nx, nz), jnp.float32)
        hrecv[...] = jnp.zeros(hrecv.shape, jnp.float32)
        pre[...] = jnp.zeros(pre.shape, jnp.float32)
        for h in range(2):
            for c in range(3):
                mags[h, c, 0] = jnp.zeros((top, nz), jnp.float32)

        barrier = pltpu.get_barrier_semaphore()

        def greet(there, len_to, wid_to):
            @pl.when(there)
            def _():
                pl.semaphore_signal(
                    barrier, inc=1, device_id={"len": len_to, "wid": wid_to}, device_id_type=MESH
                )

        for off in range(1, count):
            greet(me + off < count, me + off, row)
            greet(me - off >= 0, me - off, row)
        greet(has_low, me, row - 1)
        greet(has_high, me, row + 1)
        greet(has_next & has_low, me + 1, row - 1)
        greet(has_prev & has_high, me - 1, row + 1)

        for x in range(nx):
            for c in range(3):
                fields[0, c, x + 1, own] = ckpt_e[c, x]
                mags[0, c, x + 1, own] = ckpt_h[c, x]
                mags[1, c, x + 1, own] = adj_h[c, x]
                ysend_hi[0, c, pl.ds(x, 1)] = ckpt_e[c, x, pl.ds(ny - 1, 1)]
            for slot, c in enumerate((0, 2)):
                ysend_lo[0, slot, pl.ds(x, 1)] = ckpt_e[c, x, pl.ds(0, 1)]
                hsend[0, slot, pl.ds(x, 1)] = ckpt_h[c, x, pl.ds(ny - 1, 1)]
                hsend[1, slot, pl.ds(x, 1)] = adj_h[c, x, pl.ds(ny - 1, 1)]

        rows = lax.broadcasted_iota(jnp.int32, (ny, nz), 0)
        signs = []
        for d in range(dom_len):
            sign = jnp.zeros((ny, nz), jnp.float32)
            for w in range(dom_wid):
                value = (2 * poling[d, w] - 1).astype(jnp.float32)
                sign = jnp.where(rows // WBLK == w, value, sign)
            signs.append(sign)
        parity = jnp.float32(1.0)
        if dom_len % 2:
            parity = (1 - 2 * (me % 2)).astype(jnp.float32)
        waves = [
            [f(math.pi * x / DOMLEN) / math.sqrt(span) for x in range(nx)] for f in (math.cos, math.sin)
        ]
        for c in range(2):
            total = jnp.zeros((ny, nz), jnp.float32)
            for d in range(dom_len):
                total = total + signs[d] * sum(waves[c][d * DOMLEN : (d + 1) * DOMLEN])
            pre_out[c] = total * parity

        greeted = (
            (count - 1)
            + has_low.astype(jnp.int32)
            + has_high.astype(jnp.int32)
            + (has_next & has_low).astype(jnp.int32)
            + (has_prev & has_high).astype(jnp.int32)
        )
        pl.semaphore_wait(barrier, greeted)

        def remote(src, dst, send, recv, len_to, wid_to):
            return pltpu.make_async_remote_copy(
                src_ref=src, dst_ref=dst, send_sem=send, recv_sem=recv,
                device_id={"len": len_to, "wid": wid_to}, device_id_type=MESH,
            )

        def halo(v):
            f = fields.at[v]
            pairs = (
                (has_next, has_prev, f.at[:, nx, own], f.at[:, 0, own], me + 1, row),
                (has_prev, has_next, f.at[pl.ds(1, 2), 1, own], f.at[pl.ds(1, 2), nx + 1, own], me - 1, row),
                (has_high, has_low, ysend_hi.at[v], yrecv_lo.at[v], me, row + 1),
                (has_low, has_high, ysend_lo.at[v], yrecv_hi.at[v], me, row - 1),
                (has_next & has_low, has_prev & has_high,
                 f.at[0, nx, pl.ds(LO, 8)], f.at[0, 0, pl.ds(top, 8)], me + 1, row - 1),
                (has_prev & has_high, has_next & has_low,
                 f.at[1, 1, pl.ds(top - 8, 8)], f.at[1, nx + 1, pl.ds(0, LO)], me - 1, row + 1),
            )
            return [
                (sends, gets, remote(src, dst, send_sem.at[v, i], recv_sem.at[v, i], lt, wt))
                for i, (sends, gets, src, dst, lt, wt) in enumerate(pairs)
            ]

        def first_halo():
            pairs = (
                (has_next, has_prev, ckpt_h.at[pl.ds(1, 2), nx - 1], mags.at[0, pl.ds(1, 2), 0, own], me + 1, row),
                (has_next, has_prev, adj_h.at[pl.ds(1, 2), nx - 1], mags.at[1, pl.ds(1, 2), 0, own], me + 1, row),
                (has_high, has_low, hsend, hrecv, me, row + 1),
            )
            return [
                (sends, gets, remote(src, dst, hsend_sem.at[i], hrecv_sem.at[i], lt, wt))
                for i, (sends, gets, src, dst, lt, wt) in enumerate(pairs)
            ]

        def prefix_copies():
            return [
                (me + off < count, me - off >= 0,
                 remote(pre_out, pre.at[off], psend_sem.at[off], precv_sem.at[off], me + off, row))
                for off in range(1, count)
            ]

        def start(copies):
            for sends, _, copy in copies:
                pl.when(sends)(copy.start)

        def arrive(copies):
            for _, gets, copy in copies:
                pl.when(gets)(copy.wait_recv)

        def leave(copies):
            for sends, _, copy in copies:
                pl.when(sends)(copy.wait_send)

        start(halo(0))
        start(first_halo())
        start(prefix_copies())

        for x in range(nx):
            value = jnp.zeros((ny, nz), jnp.float32)
            for index in range(nmat):
                value = jnp.where(material[x] == index, COURANT * inv_perm[index], value)
            coef[x] = value
        bin_row = lax.broadcasted_iota(jnp.int32, (bins, nz), 0)
        bin_lane = lax.broadcasted_iota(jnp.int32, (bins, nz), 1)
        bin_freq = jnp.zeros((bins, nz), jnp.float32)
        for k in range(bins):
            bin_freq = jnp.where(bin_row == k, freqs[k], bin_freq)
        angles = bin_freq * bin_lane.astype(jnp.float32)
        cosines, sines = jnp.cos(angles), jnp.sin(angles)
        out_g[...] = jnp.zeros(out_g.shape, jnp.float32)

        lane_h = lax.broadcasted_iota(jnp.int32, (top, nz), 1)
        row_h = lax.broadcasted_iota(jnp.int32, (top, nz), 0)
        lane = lax.broadcasted_iota(jnp.int32, (ny, nz), 1)
        half = jnp.where((row_h >= LO) | has_low, COURANT, 0.0)
        whole = pl.ds(0, top)
        above = pl.ds(1, top)
        below = pl.ds(LO - 1, ny)

        def update_h(h, v, factor):
            def unpack(x, carry):
                for c in range(3):
                    fields[v, c, x + 1, pl.ds(LO - 1, 1)] = yrecv_lo[v, c, pl.ds(x, 1)]
                for slot, c in enumerate((0, 2)):
                    fields[v, c, x + 1, pl.ds(top, 1)] = yrecv_hi[v, slot, pl.ds(x, 1)]
                return carry

            lax.fori_loop(0, nx, unpack, 0, unroll=4)

            def column(x):
                ex, ey, ez = (fields[v, c, x, whole] for c in range(3))
                ex_y, ez_y = fields[v, 0, x, above], fields[v, 2, x, above]
                ey_x, ez_x = fields[v, 1, x + 1, whole], fields[v, 2, x + 1, whole]
                curl_x = (ez_y - ez) - (zforward(ey, lane_h) - ey)
                curl_y = (zforward(ex, lane_h) - ex) - (ez_x - ez)
                curl_z = (ey_x - ey) - (ex_y - ex)
                mags[h, 0, x] = mags[h, 0, x] + factor * curl_x
                mags[h, 1, x] = mags[h, 1, x] + factor * curl_y
                mags[h, 2, x] = mags[h, 2, x] + factor * curl_z

            @pl.when(has_prev)
            def _():
                column(0)

            def body(x, carry):
                column(x)
                return carry

            lax.fori_loop(1, nx + 1, body, 0, unroll=2)

        def curl_h(h, x):
            hx, hy, hz = (mags[h, c, x, own] for c in range(3))
            hx_y, hz_y = mags[h, 0, x, below], mags[h, 2, x, below]
            hy_x, hz_x = mags[h, 1, x - 1, own], mags[h, 2, x - 1, own]
            return (
                (hz - hz_y) - (hy - zbackward(hy, lane)),
                (hx - zbackward(hx, lane)) - (hz - hz_x),
                (hy - hy_x) - (hx - hx_y),
            )

        def put(v, x, values):
            for c in range(3):
                fields[v, c, x, own] = values[c]
                ysend_hi[v, c, pl.ds(x - 1, 1)] = values[c][ny - 1 :]
            for slot, c in enumerate((0, 2)):
                ysend_lo[v, slot, pl.ds(x - 1, 1)] = values[c][:1]

        def update_e(v):
            def body(x, carry):
                curls = curl_h(0, x)
                scale = coef[x - 1]
                put(v + 1, x, [fields[v, c, x, own] + scale * curls[c] for c in range(3)])
                return carry

            lax.fori_loop(1, nx + 1, body, 0, unroll=2)

        def update_adjoint(n, held, v, turn_cos, turn_sin):
            for d in range(dom_len):

                def body(x, total):
                    now = [fields[n, c, x, own] for c in range(3)]
                    drive = envc[0, x - 1] * turn_cos + envc[1, x - 1] * turn_sin
                    driven = [held(c, x) + drive * now[c] for c in range(3)]
                    dot = driven[0] * now[0] + driven[1] * now[1] + driven[2] * now[2]
                    total = total + jnp.where(material[x - 1] == 0, dot, 0.0)
                    curls = curl_h(1, x)
                    scale = coef[x - 1]
                    put(v, x, [driven[c] - scale * curls[c] for c in range(3)])
                    return total

                prods[d] = lax.fori_loop(
                    1 + d * DOMLEN, 1 + (d + 1) * DOMLEN, body, jnp.zeros((ny, nz), jnp.float32), unroll=2
                )

        def add_gradient(n):
            norm = 1.0 / math.sqrt(DOMLEN * WBLK * nz)
            sums = jnp.zeros((1, nz), jnp.float32)
            lane_g = lax.broadcasted_iota(jnp.int32, (1, nz), 1)
            for d in range(dom_len):
                for w in range(dom_wid):
                    block = prods[d, pl.ds(w * WBLK, WBLK)]
                    partial = jnp.sum(jnp.sum(block, axis=0, keepdims=True), axis=1, keepdims=True)
                    sums = jnp.where(lane_g == d * dom_wid + w, partial * norm, sums)
            cos_n = jnp.sum(jnp.where(bin_lane == n, cosines, 0.0), axis=1, keepdims=True)
            sin_n = jnp.sum(jnp.where(bin_lane == n, sines, 0.0), axis=1, keepdims=True)
            out_g[pl.ds(0, bins)] = out_g[pl.ds(0, bins)] + cos_n * sums
            out_g[pl.ds(bins, bins)] = out_g[pl.ds(bins, bins)] - sin_n * sums

        arrive(first_halo())
        for h in range(2):
            for slot, c in enumerate((0, 2)):
                for x in range(nx):
                    mags[h, c, x + 1, pl.ds(LO - 1, 1)] = hrecv[h, slot, pl.ds(x, 1)]

        def forward(v, carry):
            arrive(halo(v))
            update_h(0, v, -half)
            update_e(v)

            @pl.when(v < STEPS - 1)
            def _():
                start(halo(v + 1))

            return carry

        lax.fori_loop(0, STEPS, forward, 0)

        arrive(prefix_copies())
        for c in range(2):
            running = jnp.zeros((ny, nz), jnp.float32)
            for off in range(count - 1, 0, -1):
                running = running + pre[off, c]
            for x in range(nx):
                running = running + signs[x // DOMLEN] * (parity * waves[c][x])
                envc[c, x] = jnp.where(material[x] == 0, running, 0.0)

        update_adjoint(
            STEPS, lambda c, x: adj_e[c, x - 1], STEPS + 1, math.cos(OMEGA * STEPS), math.sin(OMEGA * STEPS)
        )

        def backward(m, carry):
            v = STEPS + 1 + m
            n = STEPS - 1 - m
            start(halo(v))
            add_gradient(n + 1)
            turn_cos = turn_sin = jnp.float32(0.0)
            for moment in range(1, STEPS):
                turn_cos = jnp.where(n == moment, math.cos(OMEGA * moment), turn_cos)
                turn_sin = jnp.where(n == moment, math.sin(OMEGA * moment), turn_sin)
            arrive(halo(v))
            update_h(1, v, half)
            update_adjoint(n, lambda c, x: fields[v, c, x, own], v + 1, turn_cos, turn_sin)
            return carry

        lax.fori_loop(0, STEPS - 1, backward, 0)

        last = VERSIONS - 1
        start(halo(last))
        add_gradient(1)
        for x in range(nx):
            for c in range(3):
                out_e[c, x] = fields[last, c, x + 1, own]
        arrive(halo(last))
        update_h(1, last, half)
        for x in range(nx):
            for c in range(3):
                out_h[c, x] = mags[1, c, x + 1, own]

        leave(first_halo())
        leave(prefix_copies())

        def drain(v, carry):
            @pl.when(v != STEPS)
            def _():
                leave(halo(v))

            return carry

        lax.fori_loop(0, VERSIONS, drain, 0)

    f32 = jnp.float32
    vmem = pl.BlockSpec(memory_space=pltpu.VMEM)
    smem = pl.BlockSpec(memory_space=pltpu.SMEM)
    return pl.pallas_call(
        kernel,
        out_shape=(
            jax.ShapeDtypeStruct((3, nx, ny, nz), f32),
            jax.ShapeDtypeStruct((3, nx, ny, nz), f32),
            jax.ShapeDtypeStruct((2 * bins, nz), f32),
        ),
        in_specs=[vmem, vmem, vmem, vmem, vmem, smem, smem, smem],
        out_specs=(vmem, vmem, vmem),
        scratch_shapes=[
            pltpu.VMEM((VERSIONS, 3, nx + 2, top + 8, nz), f32),
            pltpu.VMEM((2, 3, nx + 1, top, nz), f32),
            pltpu.VMEM((nx, ny, nz), f32),
            pltpu.VMEM((2, nx, ny, nz), f32),
            pltpu.VMEM((dom_len, ny, nz), f32),
            pltpu.VMEM((count, 2, ny, nz), f32),
            pltpu.VMEM((2, ny, nz), f32),
            pltpu.VMEM((VERSIONS, 3, nx, nz), f32),
            pltpu.VMEM((VERSIONS, 2, nx, nz), f32),
            pltpu.VMEM((VERSIONS, 3, nx, nz), f32),
            pltpu.VMEM((VERSIONS, 2, nx, nz), f32),
            pltpu.VMEM((2, 2, nx, nz), f32),
            pltpu.VMEM((2, 2, nx, nz), f32),
            pltpu.SemaphoreType.DMA((VERSIONS, 6)),
            pltpu.SemaphoreType.DMA((VERSIONS, 6)),
            pltpu.SemaphoreType.DMA((3,)),
            pltpu.SemaphoreType.DMA((3,)),
            pltpu.SemaphoreType.DMA((count,)),
            pltpu.SemaphoreType.DMA((count,)),
        ],
        compiler_params=pltpu.CompilerParams(
            collective_id=0, has_side_effects=True, vmem_limit_bytes=48 * 1024 * 1024
        ),
    )


def solution(mesh):
    count, wcount = mesh.shape["len"], mesh.shape["wid"]

    def per_device(ckpt_e, ckpt_h, adj_e, adj_h, material, inv_perm, poling, freqs):
        nx, ny, nz = material.shape
        bins = freqs.shape[0]
        call = make_kernel(count, wcount, nx, ny, nz, bins, inv_perm.shape[0])
        adjoint_e, adjoint_h, grad = call(
            ckpt_e, ckpt_h, adj_e, adj_h, material, inv_perm, poling, freqs
        )
        dom_len, dom_wid = nx // DOMLEN, ny // WBLK
        gradient = grad[:, : dom_len * dom_wid].reshape(2, bins, dom_len, dom_wid)
        return adjoint_e, adjoint_h, gradient

    field = P(None, "len", "wid", None)
    in_specs = (field, field, field, field, P("len", "wid", None), P(), P("len", "wid"), P())
    out_specs = (field, field, P(None, None, "len", "wid"))
    return jax.shard_map(
        per_device, mesh=mesh, in_specs=in_specs, out_specs=out_specs, check_vma=False
    )
```

time: 298 us -> 92.9 us (0.31); the launches traced: 293 us -> 92.5 us
  starting transfers between devices: 186 us -> 0 us
  Pallas kernels: 0 us -> 82.7 us
  waiting for transfers between devices: 60 us -> 0 us
  other arithmetic: 19.2 us -> 0 us
  blocking collectives: 8.36 us -> 0 us
  local copies, waits for them, and re-layouts: 14.8 us -> 9.12 us
  between operations: 4.01 us -> 0.66 us
    ppermute x64 -> x0, starting transfers between devices: 186 us -> none  [shifted(): lax.ppermute(value, axis, [(source, source + steps) for source in range(l...]
    pallas_call x0 -> x1, Pallas kernels: none -> 82.7 us  [per_device(): call(ckpt_e, ckpt_h, adj_e, adj_h, material, inv_perm, poling, freqs)]
    ppermute x64 -> x0, waiting for transfers between devices: 60 us -> none  [shifted(): lax.ppermute(value, axis, [(source, source + steps) for source in range(l...]
    all_gather x1 -> x0, blocking collectives: 8.36 us -> none  [carried_in(): pieces = lax.all_gather(value, axis)]
    another operation x34 -> x0, other arithmetic: 4.77 us -> none  [the longest x16 2.36 us: curl_magnetic(): jnp.stack([ydiff_backward(comp_z, zwid_plane) - zdiff_backward(comp_y), z...]
    mul x21 -> x0, other arithmetic: 3.74 us -> none  [the longest x2 3.04 us: per_device(): adjoint_e = adjoint_e + drive[None, :, :, None] * chi * forward_field]
    add x17 -> x0, other arithmetic: 3.56 us -> none  [the longest x8 2.19 us: per_device(): adjoint_h = adjoint_h + COURANT * curl_electric(adjoint_e)]
    slice x136 -> x1, local copies, waits for them, and re-layouts: 3.58 us -> 0.08 us  [per_device(): gradient = grad[:, :dom_len * dom_wid].reshape(2, bins, dom_len, dom_wid)]
  transfers between devices with their start and end apart: 64 -> 0, of which waited for: 30 -> 0; matrix products, arithmetic and copies ran while one was open for 5% -> 0% of each run, Pallas kernels for 0% -> 0%
where the time goes in v1:
time: 92.9 us; the launch traced here: 92.5 us
  Pallas kernels  82.7 us (89%)
  local copies, waits for them, and re-layouts  9.12 us (10%)
    pallas_call x1, Pallas kernels, per_device(): call(ckpt_e, ckpt_h, adj_e, adj_h, material, inv_perm, poling, freqs)  82.7 us
    unnamed x19, local copies, waits for them, and re-layouts  8.96 us

profile of v1, /device:TPU:5, one launch (start us, length us, event | category | flops | bytes accessed | tf_op | source)
XLA Modules:
  0.0 92.5 jit_solution(1319680807356322512)
XLA Ops:
  0.6 0.0 copy-start
  0.6 1.0 %copy-done = f32[3,16,16,128]{3,2,1,0:T(8,128)S(1)} copy-done((f32[3,16,16,128]{3,2,1,0:T(8,128)S(1)}, f32[3,16,16,128]{3,2,1,0:T(8,128)}, u32[]{:S(2)}) %copy-start) | copy-done | bytes 393240
  1.6 0.0 copy-start.1
  1.6 1.0 %copy-done.1 = f32[3,16,16,128]{3,2,1,0:T(8,128)S(1)} copy-done((f32[3,16,16,128]{3,2,1,0:T(8,128)S(1)}, f32[3,16,16,128]{3,2,1,0:T(8,128)}, u32[]{:S(2)}) %copy-start.1) | copy-done | bytes 393240
  2.6 0.0 copy-start.2
  2.6 1.0 %copy-done.2 = f32[3,16,16,128]{3,2,1,0:T(8,128)S(1)} copy-done((f32[3,16,16,128]{3,2,1,0:T(8,128)S(1)}, f32[3,16,16,128]{3,2,1,0:T(8,128)}, u32[]{:S(2)}) %copy-start.2) | copy-done | bytes 393240
  3.6 0.0 copy-start.3
  3.6 1.0 %copy-done.3 = f32[3,16,16,128]{3,2,1,0:T(8,128)S(1)} copy-done((f32[3,16,16,128]{3,2,1,0:T(8,128)S(1)}, f32[3,16,16,128]{3,2,1,0:T(8,128)}, u32[]{:S(2)}) %copy-start.3) | copy-done | bytes 393240
  4.6 0.0 copy-start.4
  4.6 0.9 copy-done.4
  5.5 0.0 copy-start.5
  5.5 0.7 copy-done.5
  6.2 0.0 copy-start.6
  6.2 0.7 copy-done.6
  6.9 0.0 copy-start.7
  6.9 0.7 copy-done.7
  7.5 82.7 %shard_map.103 = (f32[3,16,16,128]{3,2,1,0:T(8,128)S(1)}, f32[3,16,16,128]{3,2,1,0:T(8,128)S(1)}, f32[16,128]{1,0:T(8,128)S(1)}) custom-call(f32[3,16,16,128]{3,2,1,0:T(8,128)S(1)} %copy-done, f32[3,16,16,128]{3,2,1,0:T(8,128)S(1)} %copy-done.1, f32[3,16,16,128]{3,2,1,0:T(8,128)S(1)} %copy-done.2, f32[3,16,16,128]{3,2,1,0:T(8,128)S(1)} %copy-done.3, ...), custom_call_target="tpu_custom_call" | custom-call | tf_op jit(solution)/shard_map/pallas_call | solution.py:405
  90.3 0.1 copy.11
  90.3 0.1 reshape.9
  90.4 0.6 copy.12
  91.0 0.7 copy.15
  91.8 0.7 copy.16
Async XLA Ops:
  0.6 1.0 %copy-start = (f32[3,16,16,128]{3,2,1,0:T(8,128)S(1)}, f32[3,16,16,128]{3,2,1,0:T(8,128)}, u32[]{:S(2)}) copy-start(f32[3,16,16,128]{3,2,1,0:T(8,128)} %ckpt_e.1) | copy-start | bytes 1179652
  1.6 1.0 %copy-start.1 = (f32[3,16,16,128]{3,2,1,0:T(8,128)S(1)}, f32[3,16,16,128]{3,2,1,0:T(8,128)}, u32[]{:S(2)}) copy-start(f32[3,16,16,128]{3,2,1,0:T(8,128)} %ckpt_h.1) | copy-start | bytes 1179652
  2.6 1.0 %copy-start.2 = (f32[3,16,16,128]{3,2,1,0:T(8,128)S(1)}, f32[3,16,16,128]{3,2,1,0:T(8,128)}, u32[]{:S(2)}) copy-start(f32[3,16,16,128]{3,2,1,0:T(8,128)} %adj_e.1) | copy-start | bytes 1179652
  3.6 1.0 %copy-start.3 = (f32[3,16,16,128]{3,2,1,0:T(8,128)S(1)}, f32[3,16,16,128]{3,2,1,0:T(8,128)}, u32[]{:S(2)}) copy-start(f32[3,16,16,128]{3,2,1,0:T(8,128)} %adj_h.1) | copy-start | bytes 1179652
  4.6 0.9 copy-start.4
  5.5 0.7 copy-start.5
  6.2 0.7 copy-start.6
  6.9 0.7 copy-start.7

commit v2 on v1

--- a/solution.py
+++ b/solution.py
@@ -32,32 +32,40 @@
     span = count * nx
 
     def kernel(
-        ckpt_e, ckpt_h, adj_e, adj_h, material, inv_perm, poling, freqs,
+        ckpt_e, ckpt_h, adj_e, adj_h, cells, inv_perm, poling, freqs,
         out_e, out_h, out_g,
-        fields, mags, coef, envc, prods, pre, pre_out,
-        ysend_hi, ysend_lo, yrecv_lo, yrecv_hi, hsend, hrecv,
-        send_sem, recv_sem, hsend_sem, hrecv_sem, psend_sem, precv_sem,
+        fields, mags, material, coef, envc, prods, pre, pre_out,
+        ysend_hi, ysend_lo, yrecv_lo, yrecv_hi, hsend, hrecv, ypad,
+        load_sem, send_sem, recv_sem, hsend_sem, hrecv_sem, psend_sem, precv_sem,
     ):
         me, row = lax.axis_index("len"), lax.axis_index("wid")
         has_prev, has_next = me > 0, me < count - 1
         has_low, has_high = row > 0, row < wcount - 1
         own = pl.ds(LO, ny)
 
+        loads = [
+            pltpu.make_async_copy(src, dst, load_sem.at[i])
+            for i, (src, dst) in enumerate((
+                (ckpt_e, fields.at[0, :, pl.ds(1, nx), own]),
+                (ckpt_h, mags.at[0, :, pl.ds(1, nx), own]),
+                (adj_h, mags.at[1, :, pl.ds(1, nx), own]),
+                (cells, material),
+                (adj_e, fields.at[VERSIONS, :, pl.ds(1, nx), own]),
+            ))
+        ]
+        for load in loads:
+            load.start()
+
         for v in range(VERSIONS):
-            if v == STEPS:
-                continue
-            for c in range(3):
-                fields[v, c, 0, own] = jnp.zeros((ny, nz), jnp.float32)
-                fields[v, c, nx + 1, own] = jnp.zeros((ny, nz), jnp.float32)
-            fields[v, 0, 0, pl.ds(top, 8)] = jnp.zeros((8, nz), jnp.float32)
-            fields[v, 1, nx + 1, pl.ds(0, LO)] = jnp.zeros((LO, nz), jnp.float32)
-            yrecv_lo[v] = jnp.zeros((3, nx, nz), jnp.float32)
-            yrecv_hi[v] = jnp.zeros((2, nx, nz), jnp.float32)
-        hrecv[...] = jnp.zeros(hrecv.shape, jnp.float32)
+            if v != STEPS:
+                fields[v, 0, 0, pl.ds(top, 8)] = jnp.zeros((8, nz), jnp.float32)
+                fields[v, 1, nx + 1, pl.ds(0, LO)] = jnp.zeros((LO, nz), jnp.float32)
         pre[...] = jnp.zeros(pre.shape, jnp.float32)
         for h in range(2):
             for c in range(3):
                 mags[h, c, 0] = jnp.zeros((top, nz), jnp.float32)
+                for x in range(nx):
+                    mags[h, c, x + 1, pl.ds(0, LO)] = jnp.zeros((LO, nz), jnp.float32)
 
         barrier = pltpu.get_barrier_semaphore()
 
@@ -75,17 +83,6 @@
         greet(has_high, me, row + 1)
         greet(has_next & has_low, me + 1, row - 1)
         greet(has_prev & has_high, me - 1, row + 1)
-
-        for x in range(nx):
-            for c in range(3):
-                fields[0, c, x + 1, own] = ckpt_e[c, x]
-                mags[0, c, x + 1, own] = ckpt_h[c, x]
-                mags[1, c, x + 1, own] = adj_h[c, x]
-                ysend_hi[0, c, pl.ds(x, 1)] = ckpt_e[c, x, pl.ds(ny - 1, 1)]
-            for slot, c in enumerate((0, 2)):
-                ysend_lo[0, slot, pl.ds(x, 1)] = ckpt_e[c, x, pl.ds(0, 1)]
-                hsend[0, slot, pl.ds(x, 1)] = ckpt_h[c, x, pl.ds(ny - 1, 1)]
-                hsend[1, slot, pl.ds(x, 1)] = adj_h[c, x, pl.ds(ny - 1, 1)]
 
         rows = lax.broadcasted_iota(jnp.int32, (ny, nz), 0)
         signs = []
@@ -169,10 +166,22 @@
             for sends, _, copy in copies:
                 pl.when(sends)(copy.wait_send)
 
+        for load in loads[:3]:
+            load.wait()
+        for x in range(nx):
+            at, end = pl.ds(x, 1), pl.ds(top - 1, 1)
+            for c in range(3):
+                ysend_hi[0, c, at] = fields[0, c, x + 1, end]
+            for slot, c in enumerate((0, 2)):
+                ysend_lo[0, slot, at] = fields[0, c, x + 1, pl.ds(LO, 1)]
+                hsend[0, slot, at] = mags[0, c, x + 1, end]
+                hsend[1, slot, at] = mags[1, c, x + 1, end]
         start(halo(0))
         start(first_halo())
         start(prefix_copies())
 
+        loads[3].wait()
+        loads[4].wait()
         for x in range(nx):
             value = jnp.zeros((ny, nz), jnp.float32)
             for index in range(nmat):
@@ -187,44 +196,72 @@
         cosines, sines = jnp.cos(angles), jnp.sin(angles)
         out_g[...] = jnp.zeros(out_g.shape, jnp.float32)
 
-        lane_h = lax.broadcasted_iota(jnp.int32, (top, nz), 1)
-        row_h = lax.broadcasted_iota(jnp.int32, (top, nz), 0)
         lane = lax.broadcasted_iota(jnp.int32, (ny, nz), 1)
-        half = jnp.where((row_h >= LO) | has_low, COURANT, 0.0)
-        whole = pl.ds(0, top)
-        above = pl.ds(1, top)
+        lane_x = lax.broadcasted_iota(jnp.int32, (nx, nz), 1)
+        above = pl.ds(LO + 1, ny)
         below = pl.ds(LO - 1, ny)
 
-        def update_h(h, v, factor):
-            def unpack(x, carry):
+        def curl_e(v, x, ey_x, ez_x):
+            ex, ey, ez = (fields[v, c, x, own] for c in range(3))
+            ex_y = jnp.where(rows < ny - 1, fields[v, 0, x, above], 0.0)
+            ez_y = jnp.where(rows < ny - 1, fields[v, 2, x, above], 0.0)
+            return (
+                (ez_y - ez) - (zforward(ey, lane) - ey),
+                (zforward(ex, lane) - ex) - (ez_x - ez),
+                (ey_x - ey) - (ex_y - ex),
+            )
+
+        def inner_h(h, v, factor):
+            def add(x, curls):
                 for c in range(3):
-                    fields[v, c, x + 1, pl.ds(LO - 1, 1)] = yrecv_lo[v, c, pl.ds(x, 1)]
-                for slot, c in enumerate((0, 2)):
-                    fields[v, c, x + 1, pl.ds(top, 1)] = yrecv_hi[v, slot, pl.ds(x, 1)]
+                    mags[h, c, x, own] = mags[h, c, x, own] + factor * curls[c]
+
+            def body(x, carry):
+                add(x, curl_e(v, x, fields[v, 1, x + 1, own], fields[v, 2, x + 1, own]))
                 return carry
 
-            lax.fori_loop(0, nx, unpack, 0, unroll=4)
-
-            def column(x):
-                ex, ey, ez = (fields[v, c, x, whole] for c in range(3))
-                ex_y, ez_y = fields[v, 0, x, above], fields[v, 2, x, above]
-                ey_x, ez_x = fields[v, 1, x + 1, whole], fields[v, 2, x + 1, whole]
-                curl_x = (ez_y - ez) - (zforward(ey, lane_h) - ey)
-                curl_y = (zforward(ex, lane_h) - ex) - (ez_x - ez)
-                curl_z = (ey_x - ey) - (ex_y - ex)
-                mags[h, 0, x] = mags[h, 0, x] + factor * curl_x
-                mags[h, 1, x] = mags[h, 1, x] + factor * curl_y
-                mags[h, 2, x] = mags[h, 2, x] + factor * curl_z
+            lax.fori_loop(1, nx, body, 0, unroll=nx - 1)
+            zero = jnp.zeros((ny, nz), jnp.float32)
+            add(nx, curl_e(v, nx, zero, zero))
+
+        def edge_h(h, v, factor):
+            @pl.when(has_next)
+            def _():
+                mags[h, 1, nx, own] = mags[h, 1, nx, own] - factor * fields[v, 2, nx + 1, own]
+                mags[h, 2, nx, own] = mags[h, 2, nx, own] + factor * fields[v, 1, nx + 1, own]
+
+            @pl.when(has_high)
+            def _():
+                end = pl.ds(top - 1, 1)
+                for x in range(nx):
+                    at = pl.ds(x, 1)
+                    mags[h, 0, x + 1, end] = mags[h, 0, x + 1, end] + factor * yrecv_hi[v, 1, at]
+                    mags[h, 2, x + 1, end] = mags[h, 2, x + 1, end] - factor * yrecv_hi[v, 0, at]
 
             @pl.when(has_prev)
             def _():
-                column(0)
-
-            def body(x, carry):
-                column(x)
-                return carry
-
-            lax.fori_loop(1, nx + 1, body, 0, unroll=2)
+                ex, ey, ez = (fields[v, c, 0, own] for c in range(3))
+                curl_y = (zforward(ex, lane) - ex) - (fields[v, 2, 1, own] - ez)
+                curl_z = (fields[v, 1, 1, own] - ey) - (fields[v, 0, 0, above] - ex)
+                mags[h, 1, 0, own] = mags[h, 1, 0, own] + factor * curl_y
+                mags[h, 2, 0, own] = mags[h, 2, 0, own] + factor * curl_z
+
+            @pl.when(has_low)
+            def _():
+                ex, ey, ez = (yrecv_lo[v, c] for c in range(3))
+                ypad[pl.ds(0, nx)] = ey
+                ypad[pl.ds(nx, 1)] = fields[v, 1, nx + 1, pl.ds(LO - 1, 1)]
+                ey_x = ypad[pl.ds(1, nx)]
+                curl_x = (ysend_lo[v, 1] - ez) - (zforward(ey, lane_x) - ey)
+                curl_z = (ey_x - ey) - (ysend_lo[v, 0] - ex)
+                hrecv[h, 0] = hrecv[h, 0] + factor * curl_x
+                hrecv[h, 1] = hrecv[h, 1] + factor * curl_z
+                unpack_h(h)
+
+        def unpack_h(h):
+            for slot, c in enumerate((0, 2)):
+                for x in range(nx):
+                    mags[h, c, x + 1, pl.ds(LO - 1, 1)] = hrecv[h, slot, pl.ds(x, 1)]
 
         def curl_h(h, x):
             hx, hy, hz = (mags[h, c, x, own] for c in range(3))
@@ -250,7 +287,7 @@
                 put(v + 1, x, [fields[v, c, x, own] + scale * curls[c] for c in range(3)])
                 return carry
 
-            lax.fori_loop(1, nx + 1, body, 0, unroll=2)
+            lax.fori_loop(1, nx + 1, body, 0, unroll=nx)
 
         def update_adjoint(n, held, v, turn_cos, turn_sin):
             for d in range(dom_len):
@@ -267,7 +304,7 @@
                     return total
 
                 prods[d] = lax.fori_loop(
-                    1 + d * DOMLEN, 1 + (d + 1) * DOMLEN, body, jnp.zeros((ny, nz), jnp.float32), unroll=2
+                    1 + d * DOMLEN, 1 + (d + 1) * DOMLEN, body, jnp.zeros((ny, nz), jnp.float32), unroll=DOMLEN
                 )
 
         def add_gradient(n):
@@ -284,15 +321,16 @@
             out_g[pl.ds(0, bins)] = out_g[pl.ds(0, bins)] + cos_n * sums
             out_g[pl.ds(bins, bins)] = out_g[pl.ds(bins, bins)] - sin_n * sums
 
-        arrive(first_halo())
-        for h in range(2):
-            for slot, c in enumerate((0, 2)):
-                for x in range(nx):
-                    mags[h, c, x + 1, pl.ds(LO - 1, 1)] = hrecv[h, slot, pl.ds(x, 1)]
-
         def forward(v, carry):
+            inner_h(0, v, -COURANT)
+
+            @pl.when(v == 0)
+            def _():
+                arrive(first_halo())
+                pl.when(has_low)(lambda: unpack_h(1))
+
             arrive(halo(v))
-            update_h(0, v, -half)
+            edge_h(0, v, -COURANT)
             update_e(v)
 
             @pl.when(v < STEPS - 1)
@@ -313,7 +351,7 @@
                 envc[c, x] = jnp.where(material[x] == 0, running, 0.0)
 
         update_adjoint(
-            STEPS, lambda c, x: adj_e[c, x - 1], STEPS + 1, math.cos(OMEGA * STEPS), math.sin(OMEGA * STEPS)
+            STEPS, lambda c, x: fields[VERSIONS, c, x, own], STEPS + 1, math.cos(OMEGA * STEPS), math.sin(OMEGA * STEPS)
         )
 
         def backward(m, carry):
@@ -325,8 +363,9 @@
             for moment in range(1, STEPS):
                 turn_cos = jnp.where(n == moment, math.cos(OMEGA * moment), turn_cos)
                 turn_sin = jnp.where(n == moment, math.sin(OMEGA * moment), turn_sin)
+            inner_h(1, v, COURANT)
             arrive(halo(v))
-            update_h(1, v, half)
+            edge_h(1, v, COURANT)
             update_adjoint(n, lambda c, x: fields[v, c, x, own], v + 1, turn_cos, turn_sin)
             return carry
 
@@ -338,8 +377,9 @@
         for x in range(nx):
             for c in range(3):
                 out_e[c, x] = fields[last, c, x + 1, own]
+        inner_h(1, last, COURANT)
         arrive(halo(last))
-        update_h(1, last, half)
+        edge_h(1, last, COURANT)
         for x in range(nx):
             for c in range(3):
                 out_h[c, x] = mags[1, c, x + 1, own]
@@ -358,6 +398,7 @@
 
     f32 = jnp.float32
     vmem = pl.BlockSpec(memory_space=pltpu.VMEM)
+    hbm = pl.BlockSpec(memory_space=pl.ANY)
     smem = pl.BlockSpec(memory_space=pltpu.SMEM)
     return pl.pallas_call(
         kernel,
@@ -366,11 +407,12 @@
             jax.ShapeDtypeStruct((3, nx, ny, nz), f32),
             jax.ShapeDtypeStruct((2 * bins, nz), f32),
         ),
-        in_specs=[vmem, vmem, vmem, vmem, vmem, smem, smem, smem],
+        in_specs=[hbm, hbm, hbm, hbm, hbm, smem, smem, smem],
         out_specs=(vmem, vmem, vmem),
         scratch_shapes=[
-            pltpu.VMEM((VERSIONS, 3, nx + 2, top + 8, nz), f32),
+            pltpu.VMEM((VERSIONS + 1, 3, nx + 2, top + 8, nz), f32),
             pltpu.VMEM((2, 3, nx + 1, top, nz), f32),
+            pltpu.VMEM((nx, ny, nz), jnp.int32),
             pltpu.VMEM((nx, ny, nz), f32),
             pltpu.VMEM((2, nx, ny, nz), f32),
             pltpu.VMEM((dom_len, ny, nz), f32),
@@ -382,6 +424,8 @@
             pltpu.VMEM((VERSIONS, 2, nx, nz), f32),
             pltpu.VMEM((2, 2, nx, nz), f32),
             pltpu.VMEM((2, 2, nx, nz), f32),
+            pltpu.VMEM((nx + 8, nz), f32),
+            pltpu.SemaphoreType.DMA((5,)),
             pltpu.SemaphoreType.DMA((VERSIONS, 6)),
             pltpu.SemaphoreType.DMA((VERSIONS, 6)),
             pltpu.SemaphoreType.DMA((3,)),

time: 92.9 us -> 74.8 us (0.81)
  Pallas kernels: 82.7 us -> 64.7 us
    pallas_call x1, Pallas kernels: 82.7 us -> 64.7 us  [per_device(): call(ckpt_e, ckpt_h, adj_e, adj_h, material, inv_perm, poling, freqs)]
where the time goes in v2:
time: 74.8 us; the launch traced here: 74.5 us
  Pallas kernels  64.7 us (86%)
  local copies, waits for them, and re-layouts  9.12 us (12%)
    pallas_call x1, Pallas kernels, per_device(): call(ckpt_e, ckpt_h, adj_e, adj_h, material, inv_perm, poling, freqs)  64.7 us
    unnamed x19, local copies, waits for them, and re-layouts  8.96 us

profile of v2, /device:TPU:5, one launch (start us, length us, event | category | flops | bytes accessed | tf_op | source)
XLA Modules:
  0.0 74.5 jit_solution(10753362464922452834)
XLA Ops:
  0.6 0.0 copy-start
  0.6 1.0 %copy-done = f32[3,16,16,128]{3,2,1,0:T(8,128)S(1)} copy-done((f32[3,16,16,128]{3,2,1,0:T(8,128)S(1)}, f32[3,16,16,128]{3,2,1,0:T(8,128)}, u32[]{:S(2)}) %copy-start) | copy-done | bytes 393240
  1.6 0.0 copy-start.1
  1.6 1.0 %copy-done.1 = f32[3,16,16,128]{3,2,1,0:T(8,128)S(1)} copy-done((f32[3,16,16,128]{3,2,1,0:T(8,128)S(1)}, f32[3,16,16,128]{3,2,1,0:T(8,128)}, u32[]{:S(2)}) %copy-start.1) | copy-done | bytes 393240
  2.6 0.0 copy-start.2
  2.6 1.0 %copy-done.2 = f32[3,16,16,128]{3,2,1,0:T(8,128)S(1)} copy-done((f32[3,16,16,128]{3,2,1,0:T(8,128)S(1)}, f32[3,16,16,128]{3,2,1,0:T(8,128)}, u32[]{:S(2)}) %copy-start.2) | copy-done | bytes 393240
  3.6 0.0 copy-start.3
  3.6 1.0 %copy-done.3 = f32[3,16,16,128]{3,2,1,0:T(8,128)S(1)} copy-done((f32[3,16,16,128]{3,2,1,0:T(8,128)S(1)}, f32[3,16,16,128]{3,2,1,0:T(8,128)}, u32[]{:S(2)}) %copy-start.3) | copy-done | bytes 393240
  4.6 0.0 copy-start.4
  4.6 0.9 %copy-done.4 = s32[16,16,128]{2,1,0:T(8,128)S(1)} copy-done((s32[16,16,128]{2,1,0:T(8,128)S(1)}, s32[16,16,128]{2,1,0:T(8,128)}, u32[]{:S(2)}) %copy-start.4) | copy-done | bytes 131096
  5.5 0.0 copy-start.5
  5.5 0.7 copy-done.5
  6.2 0.0 copy-start.6
  6.2 0.7 copy-done.6
  6.9 0.0 copy-start.7
  6.9 0.7 copy-done.7
  7.5 64.7 %shard_map.103 = (f32[3,16,16,128]{3,2,1,0:T(8,128)S(1)}, f32[3,16,16,128]{3,2,1,0:T(8,128)S(1)}, f32[16,128]{1,0:T(8,128)S(1)}) custom-call(f32[3,16,16,128]{3,2,1,0:T(8,128)S(1)} %copy-done, f32[3,16,16,128]{3,2,1,0:T(8,128)S(1)} %copy-done.1, f32[3,16,16,128]{3,2,1,0:T(8,128)S(1)} %copy-done.2, f32[3,16,16,128]{3,2,1,0:T(8,128)S(1)} %copy-done.3, ...), custom_call_target="tpu_custom_call" | custom-call | tf_op jit(solution)/shard_map/pallas_call | solution.py:449
  72.2 0.1 copy.11
  72.3 0.1 reshape.9
  72.4 0.6 copy.12
  73.0 0.7 %copy.15 = f32[3,16,16,128]{3,2,1,0:T(8,128)} copy(f32[3,16,16,128]{3,2,1,0:T(8,128)S(1)} %get-tuple-element.15) | data formatting | bytes 786432
  73.8 0.7 %copy.16 = f32[3,16,16,128]{3,2,1,0:T(8,128)} copy(f32[3,16,16,128]{3,2,1,0:T(8,128)S(1)} %get-tuple-element.16) | data formatting | bytes 786432
Async XLA Ops:
  0.6 1.0 %copy-start = (f32[3,16,16,128]{3,2,1,0:T(8,128)S(1)}, f32[3,16,16,128]{3,2,1,0:T(8,128)}, u32[]{:S(2)}) copy-start(f32[3,16,16,128]{3,2,1,0:T(8,128)} %ckpt_e.1) | copy-start | bytes 1179652
  1.6 1.0 %copy-start.1 = (f32[3,16,16,128]{3,2,1,0:T(8,128)S(1)}, f32[3,16,16,128]{3,2,1,0:T(8,128)}, u32[]{:S(2)}) copy-start(f32[3,16,16,128]{3,2,1,0:T(8,128)} %ckpt_h.1) | copy-start | bytes 1179652
  2.6 1.0 %copy-start.2 = (f32[3,16,16,128]{3,2,1,0:T(8,128)S(1)}, f32[3,16,16,128]{3,2,1,0:T(8,128)}, u32[]{:S(2)}) copy-start(f32[3,16,16,128]{3,2,1,0:T(8,128)} %adj_e.1) | copy-start | bytes 1179652
  3.6 1.0 %copy-start.3 = (f32[3,16,16,128]{3,2,1,0:T(8,128)S(1)}, f32[3,16,16,128]{3,2,1,0:T(8,128)}, u32[]{:S(2)}) copy-start(f32[3,16,16,128]{3,2,1,0:T(8,128)} %adj_h.1) | copy-start | bytes 1179652
  4.6 0.9 %copy-start.4 = (s32[16,16,128]{2,1,0:T(8,128)S(1)}, s32[16,16,128]{2,1,0:T(8,128)}, u32[]{:S(2)}) copy-start(s32[16,16,128]{2,1,0:T(8,128)} %cells.1) | copy-start | bytes 393220
  5.5 0.7 copy-start.5
  6.2 0.7 copy-start.6
  6.9 0.7 copy-start.7

commit v3 on v2

--- a/solution.py
+++ b/solution.py
@@ -158,6 +158,12 @@
             for sends, _, copy in copies:
                 pl.when(sends)(copy.start)
 
+        def len_side(copies):
+            return [copies[i] for i in (4, 5, 0, 1)]
+
+        def wid_side(copies):
+            return copies[2:4]
+
         def arrive(copies):
             for _, gets, copy in copies:
                 pl.when(gets)(copy.wait_recv)
@@ -280,28 +286,33 @@
             for slot, c in enumerate((0, 2)):
                 ysend_lo[v, slot, pl.ds(x - 1, 1)] = values[c][:1]
 
-        def update_e(v):
+        def update_e(h, source, v, factor, sends):
+            def column(x):
+                curls = curl_h(h, x)
+                scale = coef[x - 1] * factor
+                put(v, x, [fields[source, c, x, own] + scale * curls[c] for c in range(3)])
+
             def body(x, carry):
-                curls = curl_h(0, x)
-                scale = coef[x - 1]
-                put(v + 1, x, [fields[v, c, x, own] + scale * curls[c] for c in range(3)])
+                column(x)
                 return carry
 
-            lax.fori_loop(1, nx + 1, body, 0, unroll=nx)
-
-        def update_adjoint(n, held, v, turn_cos, turn_sin):
+            column(nx)
+            column(1)
+            sends(len_side)
+            lax.fori_loop(2, nx, body, 0, unroll=nx - 2)
+            sends(wid_side)
+
+        def inject(n, held, v, turn_cos, turn_sin):
             for d in range(dom_len):
 
                 def body(x, total):
                     now = [fields[n, c, x, own] for c in range(3)]
                     drive = envc[0, x - 1] * turn_cos + envc[1, x - 1] * turn_sin
-                    driven = [held(c, x) + drive * now[c] for c in range(3)]
+                    driven = [fields[held, c, x, own] + drive * now[c] for c in range(3)]
                     dot = driven[0] * now[0] + driven[1] * now[1] + driven[2] * now[2]
-                    total = total + jnp.where(material[x - 1] == 0, dot, 0.0)
-                    curls = curl_h(1, x)
-                    scale = coef[x - 1]
-                    put(v, x, [driven[c] - scale * curls[c] for c in range(3)])
-                    return total
+                    for c in range(3):
+                        fields[v, c, x, own] = driven[c]
+                    return total + jnp.where(material[x - 1] == 0, dot, 0.0)
 
                 prods[d] = lax.fori_loop(
                     1 + d * DOMLEN, 1 + (d + 1) * DOMLEN, body, jnp.zeros((ny, nz), jnp.float32), unroll=DOMLEN
@@ -321,7 +332,21 @@
             out_g[pl.ds(0, bins)] = out_g[pl.ds(0, bins)] + cos_n * sums
             out_g[pl.ds(bins, bins)] = out_g[pl.ds(bins, bins)] - sin_n * sums
 
+        def envelope():
+            for c in range(2):
+                running = jnp.zeros((ny, nz), jnp.float32)
+                for off in range(count - 1, 0, -1):
+                    running = running + pre[off, c]
+                for x in range(nx):
+                    running = running + signs[x // DOMLEN] * (parity * waves[c][x])
+                    envc[c, x] = jnp.where(material[x] == 0, running, 0.0)
+
         def forward(v, carry):
+            @pl.when(v == 2)
+            def _():
+                arrive(prefix_copies())
+                envelope()
+
             inner_h(0, v, -COURANT)
 
             @pl.when(v == 0)
@@ -331,48 +356,38 @@
 
             arrive(halo(v))
             edge_h(0, v, -COURANT)
-            update_e(v)
-
-            @pl.when(v < STEPS - 1)
-            def _():
-                start(halo(v + 1))
-
+
+            def sends(side):
+                @pl.when(v < STEPS - 1)
+                def _():
+                    start(side(halo(v + 1)))
+
+            update_e(0, v, v + 1, 1.0, sends)
             return carry
 
         lax.fori_loop(0, STEPS, forward, 0)
 
-        arrive(prefix_copies())
-        for c in range(2):
-            running = jnp.zeros((ny, nz), jnp.float32)
-            for off in range(count - 1, 0, -1):
-                running = running + pre[off, c]
-            for x in range(nx):
-                running = running + signs[x // DOMLEN] * (parity * waves[c][x])
-                envc[c, x] = jnp.where(material[x] == 0, running, 0.0)
-
-        update_adjoint(
-            STEPS, lambda c, x: fields[VERSIONS, c, x, own], STEPS + 1, math.cos(OMEGA * STEPS), math.sin(OMEGA * STEPS)
-        )
+        inject(STEPS, VERSIONS, STEPS + 1, math.cos(OMEGA * STEPS), math.sin(OMEGA * STEPS))
+        update_e(1, STEPS + 1, STEPS + 1, -1.0, lambda side: start(side(halo(STEPS + 1))))
 
         def backward(m, carry):
             v = STEPS + 1 + m
             n = STEPS - 1 - m
-            start(halo(v))
+            inner_h(1, v, COURANT)
             add_gradient(n + 1)
             turn_cos = turn_sin = jnp.float32(0.0)
             for moment in range(1, STEPS):
                 turn_cos = jnp.where(n == moment, math.cos(OMEGA * moment), turn_cos)
                 turn_sin = jnp.where(n == moment, math.sin(OMEGA * moment), turn_sin)
-            inner_h(1, v, COURANT)
+            inject(n, v, v + 1, turn_cos, turn_sin)
             arrive(halo(v))
             edge_h(1, v, COURANT)
-            update_adjoint(n, lambda c, x: fields[v, c, x, own], v + 1, turn_cos, turn_sin)
+            update_e(1, v + 1, v + 1, -1.0, lambda side: start(side(halo(v + 1))))
             return carry
 
         lax.fori_loop(0, STEPS - 1, backward, 0)
 
         last = VERSIONS - 1
-        start(halo(last))
         add_gradient(1)
         for x in range(nx):
             for c in range(3):
@@ -434,7 +449,7 @@
             pltpu.SemaphoreType.DMA((count,)),
         ],
         compiler_params=pltpu.CompilerParams(
-            collective_id=0, has_side_effects=True, vmem_limit_bytes=48 * 1024 * 1024
+            collective_id=0, has_side_effects=True, vmem_limit_bytes=63 * 1024 * 1024
         ),
     )
 

time: 74.8 us -> 66.2 us (0.89)
  local copies, waits for them, and re-layouts: 9.12 us -> 4.03 us
  Pallas kernels: 64.7 us -> 60.9 us
    unnamed x19 -> x5, local copies, waits for them, and re-layouts: 8.96 us -> 3.17 us
    pallas_call x1, Pallas kernels: 64.7 us -> 60.9 us  [per_device(): call(ckpt_e, ckpt_h, adj_e, adj_h, material, inv_perm, poling, freqs)]
where the time goes in v3:
time: 66.2 us; the launch traced here: 65.5 us
  Pallas kernels  60.9 us (92%)
  local copies, waits for them, and re-layouts  4.03 us (6%)
    pallas_call x1, Pallas kernels, per_device(): call(ckpt_e, ckpt_h, adj_e, adj_h, material, inv_perm, poling, freqs)  60.9 us
    unnamed x5, local copies, waits for them, and re-layouts  3.17 us

profile of v3, /device:TPU:5, one launch (start us, length us, event | category | flops | bytes accessed | tf_op | source)
XLA Modules:
  0.0 65.5 jit_solution(2241316330900520720)
XLA Ops:
  0.6 60.9 %shard_map.103 = (f32[3,16,16,128]{3,2,1,0:T(8,128)}, f32[3,16,16,128]{3,2,1,0:T(8,128)}, f32[16,128]{1,0:T(8,128)}) custom-call(f32[3,16,16,128]{3,2,1,0:T(8,128)} %ckpt_e.1, f32[3,16,16,128]{3,2,1,0:T(8,128)} %ckpt_h.1, f32[3,16,16,128]{3,2,1,0:T(8,128)} %adj_e.1, f32[3,16,16,128]{3,2,1,0:T(8,128)} %adj_h.1, s32[16,16,128]{2,1,0:T(8,128)} %cells.1, ...), custom_call_target="tpu_custom_call" | custom-call | tf_op jit(solution)/shard_map/pallas_call | solution.py:464
  61.5 0.8 %copy.11 = f32[16,4]{0,1:T(4,128)S(1)} copy(f32[16,4]{1,0:T(8,128)} %bitcast.3) | data formatting | bytes 512 | tf_op jit(solution)/shard_map/slice | solution.py:468
  62.3 0.1 reshape.9
  62.4 0.6 copy.12
  63.0 0.0 copy-start
  63.0 1.8 %copy.15 = f32[3,16,16,128]{3,2,1,0:T(8,128)} copy(f32[3,16,16,128]{3,2,1,0:T(8,128)} %get-tuple-element.15) | data formatting | bytes 786432
  64.8 0.0 copy-done
  64.8 0.7 %copy.16 = f32[3,16,16,128]{3,2,1,0:T(8,128)} copy(f32[3,16,16,128]{3,2,1,0:T(8,128)S(1)} %copy-done) | data formatting | bytes 786432
Async XLA Ops:
  63.0 1.8 %copy-start = (f32[3,16,16,128]{3,2,1,0:T(8,128)S(1)}, f32[3,16,16,128]{3,2,1,0:T(8,128)}, u32[]{:S(2)}) copy-start(f32[3,16,16,128]{3,2,1,0:T(8,128)} %get-tuple-element.16) | copy-start | bytes 1179652

commit v4 on v3

--- a/solution.py
+++ b/solution.py
@@ -35,7 +35,7 @@
         ckpt_e, ckpt_h, adj_e, adj_h, cells, inv_perm, poling, freqs,
         out_e, out_h, out_g,
         fields, mags, material, coef, envc, prods, pre, pre_out,
-        ysend_hi, ysend_lo, yrecv_lo, yrecv_hi, hsend, hrecv, ypad,
+        ysend_hi, ysend_lo, yrecv_lo, yrecv_hi, hsend, hrecv, ypad, waves_g, coef_rows,
         load_sem, send_sem, recv_sem, hsend_sem, hrecv_sem, psend_sem, precv_sem,
     ):
         me, row = lax.axis_index("len"), lax.axis_index("wid")
@@ -158,12 +158,6 @@
             for sends, _, copy in copies:
                 pl.when(sends)(copy.start)
 
-        def len_side(copies):
-            return [copies[i] for i in (4, 5, 0, 1)]
-
-        def wid_side(copies):
-            return copies[2:4]
-
         def arrive(copies):
             for _, gets, copy in copies:
                 pl.when(gets)(copy.wait_recv)
@@ -193,17 +187,20 @@
             for index in range(nmat):
                 value = jnp.where(material[x] == index, COURANT * inv_perm[index], value)
             coef[x] = value
-        bin_row = lax.broadcasted_iota(jnp.int32, (bins, nz), 0)
-        bin_lane = lax.broadcasted_iota(jnp.int32, (bins, nz), 1)
-        bin_freq = jnp.zeros((bins, nz), jnp.float32)
+            coef_rows[0, pl.ds(x, 1)] = value[:1]
+            coef_rows[1, pl.ds(x, 1)] = value[ny - 1 :]
+        bin_row = lax.broadcasted_iota(jnp.int32, (STEPS, nz), 0)
+        bin_lane = lax.broadcasted_iota(jnp.int32, (STEPS, nz), 1)
+        bin_freq = jnp.zeros((STEPS, nz), jnp.float32)
         for k in range(bins):
-            bin_freq = jnp.where(bin_row == k, freqs[k], bin_freq)
-        angles = bin_freq * bin_lane.astype(jnp.float32)
-        cosines, sines = jnp.cos(angles), jnp.sin(angles)
+            bin_freq = jnp.where(bin_lane == k, freqs[k], bin_freq)
+        angles = bin_freq * (bin_row + 1).astype(jnp.float32)
+        waves_g[0], waves_g[1] = jnp.cos(angles), -jnp.sin(angles)
         out_g[...] = jnp.zeros(out_g.shape, jnp.float32)
 
         lane = lax.broadcasted_iota(jnp.int32, (ny, nz), 1)
         lane_x = lax.broadcasted_iota(jnp.int32, (nx, nz), 1)
+        rows_x = lax.broadcasted_iota(jnp.int32, (nx, nz), 0)
         above = pl.ds(LO + 1, ny)
         below = pl.ds(LO - 1, ny)
 
@@ -286,21 +283,84 @@
             for slot, c in enumerate((0, 2)):
                 ysend_lo[v, slot, pl.ds(x - 1, 1)] = values[c][:1]
 
-        def update_e(h, source, v, factor, sends):
-            def column(x):
+        def update_e(h, source, v, factor):
+            def body(x, carry):
                 curls = curl_h(h, x)
                 scale = coef[x - 1] * factor
                 put(v, x, [fields[source, c, x, own] + scale * curls[c] for c in range(3)])
-
-            def body(x, carry):
-                column(x)
                 return carry
 
-            column(nx)
-            column(1)
-            sends(len_side)
-            lax.fori_loop(2, nx, body, 0, unroll=nx - 2)
-            sends(wid_side)
+            lax.fori_loop(1, nx + 1, body, 0, unroll=nx)
+
+        def edge_e(h, v, factor, new, factor_e):
+            @pl.when(has_next)
+            def _():
+                dy, dz = -factor * fields[v, 2, nx + 1, own], factor * fields[v, 1, nx + 1, own]
+                mags[h, 1, nx, own] = mags[h, 1, nx, own] + dy
+                mags[h, 2, nx, own] = mags[h, 2, nx, own] + dz
+                dz_y = jnp.where(rows > 0, pltpu.roll(dz, 1, 0), 0.0)
+                scale = coef[nx - 1] * factor_e
+                curls = ((dz - dz_y) - (dy - zbackward(dy, lane)), -dz, dy)
+                for c in range(3):
+                    fields[new, c, nx, own] = fields[new, c, nx, own] + scale * curls[c]
+
+            @pl.when(has_prev)
+            def _():
+                ex, ey, ez = (fields[v, c, 0, own] for c in range(3))
+                dy = factor * ((zforward(ex, lane) - ex) - (fields[v, 2, 1, own] - ez))
+                dz = factor * ((fields[v, 1, 1, own] - ey) - (fields[v, 0, 0, above] - ex))
+                mags[h, 1, 0, own] = mags[h, 1, 0, own] + dy
+                mags[h, 2, 0, own] = mags[h, 2, 0, own] + dz
+                scale = coef[0] * factor_e
+                fields[new, 1, 1, own] = fields[new, 1, 1, own] + scale * dz
+                fields[new, 2, 1, own] = fields[new, 2, 1, own] - scale * dy
+
+            end, begin = pl.ds(top - 1, 1), pl.ds(LO, 1)
+            for x in (0, nx - 1):
+                for c in range(3):
+                    ysend_hi[new, c, pl.ds(x, 1)] = fields[new, c, x + 1, end]
+                for slot, c in enumerate((0, 2)):
+                    ysend_lo[new, slot, pl.ds(x, 1)] = fields[new, c, x + 1, begin]
+
+            @pl.when(has_high)
+            def _():
+                dx, dz = factor * yrecv_hi[v, 1], -factor * yrecv_hi[v, 0]
+                dz_x = jnp.where(rows_x > 0, pltpu.roll(dz, 1, 0), 0.0)
+                scale = coef_rows[1] * factor_e
+                curls = (dz, (dx - zbackward(dx, lane_x)) - (dz - dz_x), -dx)
+                for c in range(3):
+                    ysend_hi[new, c] = ysend_hi[new, c] + scale * curls[c]
+                for c in range(3):
+                    for x in range(nx):
+                        fields[new, c, x + 1, end] = ysend_hi[new, c, pl.ds(x, 1)]
+
+            @pl.when(has_low)
+            def _():
+                ex, ey, ez = (yrecv_lo[v, c] for c in range(3))
+                ypad[pl.ds(0, nx)] = ey
+                ypad[pl.ds(nx, 1)] = fields[v, 1, nx + 1, pl.ds(LO - 1, 1)]
+                ey_x = ypad[pl.ds(1, nx)]
+                dx = factor * ((ysend_lo[v, 1] - ez) - (zforward(ey, lane_x) - ey))
+                dz = factor * ((ey_x - ey) - (ysend_lo[v, 0] - ex))
+                hrecv[h, 0] = hrecv[h, 0] + dx
+                hrecv[h, 1] = hrecv[h, 1] + dz
+                scale = coef_rows[0] * factor_e
+                ysend_lo[new, 0] = ysend_lo[new, 0] - scale * dz
+                ysend_lo[new, 1] = ysend_lo[new, 1] + scale * dx
+                for slot, c in enumerate((0, 2)):
+                    for x in range(nx):
+                        fields[new, c, x + 1, begin] = ysend_lo[new, slot, pl.ds(x, 1)]
+
+        def edge_rows(h, v, factor):
+            @pl.when(has_high)
+            def _():
+                end = pl.ds(top - 1, 1)
+                for x in range(nx):
+                    at = pl.ds(x, 1)
+                    mags[h, 0, x + 1, end] = mags[h, 0, x + 1, end] + factor * yrecv_hi[v, 1, at]
+                    mags[h, 2, x + 1, end] = mags[h, 2, x + 1, end] - factor * yrecv_hi[v, 0, at]
+
+            pl.when(has_low)(lambda: unpack_h(h))
 
         def inject(n, held, v, turn_cos, turn_sin):
             for d in range(dom_len):
@@ -320,17 +380,14 @@
 
         def add_gradient(n):
             norm = 1.0 / math.sqrt(DOMLEN * WBLK * nz)
-            sums = jnp.zeros((1, nz), jnp.float32)
-            lane_g = lax.broadcasted_iota(jnp.int32, (1, nz), 1)
+            at = pl.ds(n - 1, 1)
             for d in range(dom_len):
                 for w in range(dom_wid):
                     block = prods[d, pl.ds(w * WBLK, WBLK)]
-                    partial = jnp.sum(jnp.sum(block, axis=0, keepdims=True), axis=1, keepdims=True)
-                    sums = jnp.where(lane_g == d * dom_wid + w, partial * norm, sums)
-            cos_n = jnp.sum(jnp.where(bin_lane == n, cosines, 0.0), axis=1, keepdims=True)
-            sin_n = jnp.sum(jnp.where(bin_lane == n, sines, 0.0), axis=1, keepdims=True)
-            out_g[pl.ds(0, bins)] = out_g[pl.ds(0, bins)] + cos_n * sums
-            out_g[pl.ds(bins, bins)] = out_g[pl.ds(bins, bins)] - sin_n * sums
+                    partial = jnp.sum(jnp.sum(block, axis=0, keepdims=True), axis=1, keepdims=True) * norm
+                    for c in range(2):
+                        term = (waves_g[c, at] * partial)[:, :bins]
+                        out_g[c, d, pl.ds(w, 1)] = out_g[c, d, pl.ds(w, 1)] + term
 
         def envelope():
             for c in range(2):
@@ -352,23 +409,28 @@
             @pl.when(v == 0)
             def _():
                 arrive(first_halo())
-                pl.when(has_low)(lambda: unpack_h(1))
-
+
+                @pl.when(has_low)
+                def _():
+                    unpack_h(0)
+                    unpack_h(1)
+
+            update_e(0, v, v + 1, 1.0)
             arrive(halo(v))
-            edge_h(0, v, -COURANT)
-
-            def sends(side):
-                @pl.when(v < STEPS - 1)
-                def _():
-                    start(side(halo(v + 1)))
-
-            update_e(0, v, v + 1, 1.0, sends)
+            edge_e(0, v, -COURANT, v + 1, 1.0)
+
+            @pl.when(v < STEPS - 1)
+            def _():
+                start(halo(v + 1))
+
+            edge_rows(0, v, -COURANT)
             return carry
 
         lax.fori_loop(0, STEPS, forward, 0)
 
         inject(STEPS, VERSIONS, STEPS + 1, math.cos(OMEGA * STEPS), math.sin(OMEGA * STEPS))
-        update_e(1, STEPS + 1, STEPS + 1, -1.0, lambda side: start(side(halo(STEPS + 1))))
+        update_e(1, STEPS + 1, STEPS + 1, -1.0)
+        start(halo(STEPS + 1))
 
         def backward(m, carry):
             v = STEPS + 1 + m
@@ -380,9 +442,11 @@
                 turn_cos = jnp.where(n == moment, math.cos(OMEGA * moment), turn_cos)
                 turn_sin = jnp.where(n == moment, math.sin(OMEGA * moment), turn_sin)
             inject(n, v, v + 1, turn_cos, turn_sin)
+            update_e(1, v + 1, v + 1, -1.0)
             arrive(halo(v))
-            edge_h(1, v, COURANT)
-            update_e(1, v + 1, v + 1, -1.0, lambda side: start(side(halo(v + 1))))
+            edge_e(1, v, COURANT, v + 1, -1.0)
+            start(halo(v + 1))
+            edge_rows(1, v, COURANT)
             return carry
 
         lax.fori_loop(0, STEPS - 1, backward, 0)
@@ -420,7 +484,7 @@
         out_shape=(
             jax.ShapeDtypeStruct((3, nx, ny, nz), f32),
             jax.ShapeDtypeStruct((3, nx, ny, nz), f32),
-            jax.ShapeDtypeStruct((2 * bins, nz), f32),
+            jax.ShapeDtypeStruct((2, dom_len, dom_wid, bins), f32),
         ),
         in_specs=[hbm, hbm, hbm, hbm, hbm, smem, smem, smem],
         out_specs=(vmem, vmem, vmem),
@@ -440,6 +504,8 @@
             pltpu.VMEM((2, 2, nx, nz), f32),
             pltpu.VMEM((2, 2, nx, nz), f32),
             pltpu.VMEM((nx + 8, nz), f32),
+            pltpu.VMEM((2, STEPS, nz), f32),
+            pltpu.VMEM((2, nx, nz), f32),
             pltpu.SemaphoreType.DMA((5,)),
             pltpu.SemaphoreType.DMA((VERSIONS, 6)),
             pltpu.SemaphoreType.DMA((VERSIONS, 6)),
@@ -464,8 +530,7 @@
         adjoint_e, adjoint_h, grad = call(
             ckpt_e, ckpt_h, adj_e, adj_h, material, inv_perm, poling, freqs
         )
-        dom_len, dom_wid = nx // DOMLEN, ny // WBLK
-        gradient = grad[:, : dom_len * dom_wid].reshape(2, bins, dom_len, dom_wid)
+        gradient = jnp.transpose(grad, (0, 3, 1, 2))
         return adjoint_e, adjoint_h, gradient
 
     field = P(None, "len", "wid", None)

time: 66.2 us -> 68.8 us (1.039)
  Pallas kernels: 60.9 us -> 64.8 us
  local copies, waits for them, and re-layouts: 4.03 us -> 3.16 us
    pallas_call x1, Pallas kernels: 60.9 us -> 64.8 us  [per_device(): call(ckpt_e, ckpt_h, adj_e, adj_h, material, inv_perm, poling, freqs)]
    slice x1 -> x0, local copies, waits for them, and re-layouts: 0.78 us -> none  [per_device(): gradient = grad[:, :dom_len * dom_wid].reshape(2, bins, dom_len, dom_wid)]
    unnamed x5 -> x7, local copies, waits for them, and re-layouts: 3.17 us -> 3.16 us
where the time goes in v4:
time: 68.8 us; the launch traced here: 68.6 us
  Pallas kernels  64.8 us (94%)
  local copies, waits for them, and re-layouts  3.16 us (5%)
    pallas_call x1, Pallas kernels, per_device(): call(ckpt_e, ckpt_h, adj_e, adj_h, material, inv_perm, poling, freqs)  64.8 us
    unnamed x7, local copies, waits for them, and re-layouts  3.16 us

profile of v4, /device:TPU:5, one launch (start us, length us, event | category | flops | bytes accessed | tf_op | source)
XLA Modules:
  0.0 68.6 jit_solution(11846551845322734844)
XLA Ops:
  0.6 64.8 %shard_map.103 = (f32[3,16,16,128]{3,2,1,0:T(8,128)}, f32[3,16,16,128]{3,2,1,0:T(8,128)}, f32[2,2,2,8]{3,2,1,0:T(2,128)}) custom-call(f32[3,16,16,128]{3,2,1,0:T(8,128)} %ckpt_e.1, f32[3,16,16,128]{3,2,1,0:T(8,128)} %ckpt_h.1, f32[3,16,16,128]{3,2,1,0:T(8,128)} %adj_e.1, f32[3,16,16,128]{3,2,1,0:T(8,128)} %adj_h.1, s32[16,16,128]{2,1,0:T(8,128)} %cells.1, ...), custom_call_target="tpu_custom_call" | custom-call | tf_op jit(solution)/shard_map/pallas_call | solution.py:530
  65.4 0.0 copy-start
  65.4 1.8 %copy.14 = f32[3,16,16,128]{3,2,1,0:T(8,128)} copy(f32[3,16,16,128]{3,2,1,0:T(8,128)} %get-tuple-element.12) | data formatting | bytes 786432
  67.2 0.0 copy-done
  67.2 0.0 copy-start.1
  67.2 0.7 %copy.15 = f32[3,16,16,128]{3,2,1,0:T(8,128)} copy(f32[3,16,16,128]{3,2,1,0:T(8,128)S(1)} %copy-done) | data formatting | bytes 786432
  68.0 0.0 copy-done.1
  68.0 0.6 copy.16
Async XLA Ops:
  65.4 1.8 %copy-start = (f32[3,16,16,128]{3,2,1,0:T(8,128)S(1)}, f32[3,16,16,128]{3,2,1,0:T(8,128)}, u32[]{:S(2)}) copy-start(f32[3,16,16,128]{3,2,1,0:T(8,128)} %get-tuple-element.13) | copy-start | bytes 1179652
  67.2 0.8 %copy-start.1 = (f32[2,2,2,8]{3,2,1,0:T(2,128)S(1)}, f32[2,2,2,8]{3,2,1,0:T(2,128)}, u32[]{:S(2)}) copy-start(f32[2,2,2,8]{3,2,1,0:T(2,128)} %get-tuple-element.8) | copy-start | bytes 772

commit v5 on v3

--- a/solution.py
+++ b/solution.py
@@ -35,7 +35,7 @@
         ckpt_e, ckpt_h, adj_e, adj_h, cells, inv_perm, poling, freqs,
         out_e, out_h, out_g,
         fields, mags, material, coef, envc, prods, pre, pre_out,
-        ysend_hi, ysend_lo, yrecv_lo, yrecv_hi, hsend, hrecv, ypad,
+        ysend_hi, ysend_lo, yrecv_lo, yrecv_hi, hsend, hrecv, ypad, waves_g,
         load_sem, send_sem, recv_sem, hsend_sem, hrecv_sem, psend_sem, precv_sem,
     ):
         me, row = lax.axis_index("len"), lax.axis_index("wid")
@@ -193,13 +193,13 @@
             for index in range(nmat):
                 value = jnp.where(material[x] == index, COURANT * inv_perm[index], value)
             coef[x] = value
-        bin_row = lax.broadcasted_iota(jnp.int32, (bins, nz), 0)
-        bin_lane = lax.broadcasted_iota(jnp.int32, (bins, nz), 1)
-        bin_freq = jnp.zeros((bins, nz), jnp.float32)
+        bin_row = lax.broadcasted_iota(jnp.int32, (STEPS, nz), 0)
+        bin_lane = lax.broadcasted_iota(jnp.int32, (STEPS, nz), 1)
+        bin_freq = jnp.zeros((STEPS, nz), jnp.float32)
         for k in range(bins):
-            bin_freq = jnp.where(bin_row == k, freqs[k], bin_freq)
-        angles = bin_freq * bin_lane.astype(jnp.float32)
-        cosines, sines = jnp.cos(angles), jnp.sin(angles)
+            bin_freq = jnp.where(bin_lane == k, freqs[k], bin_freq)
+        angles = bin_freq * (bin_row + 1).astype(jnp.float32)
+        waves_g[0], waves_g[1] = jnp.cos(angles), -jnp.sin(angles)
         out_g[...] = jnp.zeros(out_g.shape, jnp.float32)
 
         lane = lax.broadcasted_iota(jnp.int32, (ny, nz), 1)
@@ -320,17 +320,14 @@
 
         def add_gradient(n):
             norm = 1.0 / math.sqrt(DOMLEN * WBLK * nz)
-            sums = jnp.zeros((1, nz), jnp.float32)
-            lane_g = lax.broadcasted_iota(jnp.int32, (1, nz), 1)
+            at = pl.ds(n - 1, 1)
             for d in range(dom_len):
                 for w in range(dom_wid):
                     block = prods[d, pl.ds(w * WBLK, WBLK)]
-                    partial = jnp.sum(jnp.sum(block, axis=0, keepdims=True), axis=1, keepdims=True)
-                    sums = jnp.where(lane_g == d * dom_wid + w, partial * norm, sums)
-            cos_n = jnp.sum(jnp.where(bin_lane == n, cosines, 0.0), axis=1, keepdims=True)
-            sin_n = jnp.sum(jnp.where(bin_lane == n, sines, 0.0), axis=1, keepdims=True)
-            out_g[pl.ds(0, bins)] = out_g[pl.ds(0, bins)] + cos_n * sums
-            out_g[pl.ds(bins, bins)] = out_g[pl.ds(bins, bins)] - sin_n * sums
+                    partial = jnp.sum(jnp.sum(block, axis=0, keepdims=True), axis=1, keepdims=True) * norm
+                    for c in range(2):
+                        term = (waves_g[c, at] * partial)[:, :bins]
+                        out_g[c, d, pl.ds(w, 1)] = out_g[c, d, pl.ds(w, 1)] + term
 
         def envelope():
             for c in range(2):
@@ -420,7 +417,7 @@
         out_shape=(
             jax.ShapeDtypeStruct((3, nx, ny, nz), f32),
             jax.ShapeDtypeStruct((3, nx, ny, nz), f32),
-            jax.ShapeDtypeStruct((2 * bins, nz), f32),
+            jax.ShapeDtypeStruct((2, dom_len, dom_wid, bins), f32),
         ),
         in_specs=[hbm, hbm, hbm, hbm, hbm, smem, smem, smem],
         out_specs=(vmem, vmem, vmem),
@@ -440,6 +437,7 @@
             pltpu.VMEM((2, 2, nx, nz), f32),
             pltpu.VMEM((2, 2, nx, nz), f32),
             pltpu.VMEM((nx + 8, nz), f32),
+            pltpu.VMEM((2, STEPS, nz), f32),
             pltpu.SemaphoreType.DMA((5,)),
             pltpu.SemaphoreType.DMA((VERSIONS, 6)),
             pltpu.SemaphoreType.DMA((VERSIONS, 6)),
@@ -464,8 +462,7 @@
         adjoint_e, adjoint_h, grad = call(
             ckpt_e, ckpt_h, adj_e, adj_h, material, inv_perm, poling, freqs
         )
-        dom_len, dom_wid = nx // DOMLEN, ny // WBLK
-        gradient = grad[:, : dom_len * dom_wid].reshape(2, bins, dom_len, dom_wid)
+        gradient = jnp.transpose(grad, (0, 3, 1, 2))
         return adjoint_e, adjoint_h, gradient
 
     field = P(None, "len", "wid", None)

time: 66.2 us -> 65.3 us (0.986)
  local copies, waits for them, and re-layouts: 4.03 us -> 3.16 us
    slice x1 -> x0, local copies, waits for them, and re-layouts: 0.78 us -> none  [per_device(): gradient = grad[:, :dom_len * dom_wid].reshape(2, bins, dom_len, dom_wid)]
    unnamed x5 -> x7, local copies, waits for them, and re-layouts: 3.17 us -> 3.16 us
where the time goes in v5:
time: 65.3 us; the launch traced here: 64.7 us
  Pallas kernels  60.9 us (93%)
  local copies, waits for them, and re-layouts  3.16 us (5%)
    pallas_call x1, Pallas kernels, per_device(): call(ckpt_e, ckpt_h, adj_e, adj_h, material, inv_perm, poling, freqs)  60.9 us
    unnamed x7, local copies, waits for them, and re-layouts  3.16 us

profile of v5, /device:TPU:5, one launch (start us, length us, event | category | flops | bytes accessed | tf_op | source)
XLA Modules:
  0.0 64.7 jit_solution(17366853471437038164)
XLA Ops:
  0.6 60.9 %shard_map.103 = (f32[3,16,16,128]{3,2,1,0:T(8,128)}, f32[3,16,16,128]{3,2,1,0:T(8,128)}, f32[2,2,2,8]{3,2,1,0:T(2,128)}) custom-call(f32[3,16,16,128]{3,2,1,0:T(8,128)} %ckpt_e.1, f32[3,16,16,128]{3,2,1,0:T(8,128)} %ckpt_h.1, f32[3,16,16,128]{3,2,1,0:T(8,128)} %adj_e.1, f32[3,16,16,128]{3,2,1,0:T(8,128)} %adj_h.1, s32[16,16,128]{2,1,0:T(8,128)} %cells.1, ...), custom_call_target="tpu_custom_call" | custom-call | tf_op jit(solution)/shard_map/pallas_call | solution.py:462
  61.5 0.0 copy-start
  61.5 1.8 %copy.14 = f32[3,16,16,128]{3,2,1,0:T(8,128)} copy(f32[3,16,16,128]{3,2,1,0:T(8,128)} %get-tuple-element.12) | data formatting | bytes 786432
  63.3 0.0 copy-done
  63.3 0.0 copy-start.1
  63.3 0.7 %copy.15 = f32[3,16,16,128]{3,2,1,0:T(8,128)} copy(f32[3,16,16,128]{3,2,1,0:T(8,128)S(1)} %copy-done) | data formatting | bytes 786432
  64.1 0.0 copy-done.1
  64.1 0.6 copy.16
Async XLA Ops:
  61.5 1.8 %copy-start = (f32[3,16,16,128]{3,2,1,0:T(8,128)S(1)}, f32[3,16,16,128]{3,2,1,0:T(8,128)}, u32[]{:S(2)}) copy-start(f32[3,16,16,128]{3,2,1,0:T(8,128)} %get-tuple-element.13) | copy-start | bytes 1179652
  63.3 0.8 %copy-start.1 = (f32[2,2,2,8]{3,2,1,0:T(2,128)S(1)}, f32[2,2,2,8]{3,2,1,0:T(2,128)}, u32[]{:S(2)}) copy-start(f32[2,2,2,8]{3,2,1,0:T(2,128)} %get-tuple-element.8) | copy-start | bytes 772
